TPU v7x, 256 devices: a whole 4x4x8 slice. The times are simulated.
256 devices in a mesh: seq: 64 (over z, x, core), head: 4 (over y).
Axes of the slice: x: 4, y: 4, z: 8, core: 2. Of those that a mesh axis runs over, the one named last changes fastest.
Arguments:
- queries: bfloat16 [16384, 4096], P('seq', 'head'), may hold values from -6 to 6
- keys: bfloat16 [16384, 4096], P('seq', 'head'), may hold values from -6 to 6
- values: bfloat16 [16384, 4096], P('seq', 'head'), may hold values from -6 to 6
- outputs: bfloat16 [16384, 4096], P('seq', 'head'), may hold values from -6 to 6
- out_grad: bfloat16 [16384, 4096], P('seq', 'head'), may hold values from -6 to 6
- log_sum: float32 [32, 16384], P('head', 'seq'), may hold values from 4 to 6
- selected: int32 [32, 256, 16], P('head', 'seq'), may hold values from -1 to 255, as said below
- w_query: bfloat16 [4096, 4096], P(None, 'head'), may hold values from -0.09375 to 0.09375
Outputs:
- x_grad: bfloat16 [16384, 4096], P(('seq', 'head'))
- key_gradient: bfloat16 [16384, 4096], P('seq', 'head')
- value_gradient: bfloat16 [16384, 4096], P('seq', 'head')
Inputs may be any that keep to these rules, and one draw needn't show every extreme that they name: Row (h, b) lists distinct blocks: entry 0 is b itself, the others are blocks before b, and entries equal to -1 (unused) come last. Over the query blocks of one index of seq and the heads of one index of head, the distinct (head, block) pairs selected from the blocks of any one other index of seq number at most 2; some pair of indices reaches 2 in every draw.
All inputs are finite; a program needn't handle non-finite values.
Results may differ from a plain program's by a relative error of at most 0.0075.
Values may be sent and summed in bfloat16 or wider, within the bound.
A program may use at most 128 MiB of HBM per device.

v0:
```python
import functools

import jax
import jax.numpy as jnp
from jax import lax
from jax.experimental import pallas as pl
from jax.experimental.pallas import tpu as pltpu
from jax.sharding import PartitionSpec as P

CAP = 2
HD = 128
BLOCK = 64
FAR = 1e30

NT = (((1,), (1,)), ((), ()))
TN = (((0,), (0,)), ((), ()))


def dot(a, b, dims=(((1,), (0,)), ((), ()))):
    return lax.dot_general(a, b, dims, preferred_element_type=jnp.float32)


def request_tables(selected, me, shards):
    heads, blocks, picks = selected.shape
    units = heads * blocks
    every = jnp.arange(shards * blocks, dtype=jnp.int32)
    hit = jnp.any(selected[:, :, :, None] == every, axis=2)
    weight = (1 << jnp.arange(blocks, dtype=jnp.int32))[None, :, None]
    bits = jnp.sum(jnp.where(hit, weight, 0), axis=1)
    bits = bits.reshape(heads, shards, blocks).transpose(1, 0, 2).reshape(shards, units)
    owners = jnp.arange(shards, dtype=jnp.int32)[:, None]
    local = jnp.sum(jnp.where(owners == me, bits, 0), axis=0)
    bits = jnp.where(owners == me, 0, bits)
    index = jnp.arange(units, dtype=jnp.int32)
    first = jnp.min(jnp.where(bits > 0, index, units), axis=1, keepdims=True)
    second = jnp.min(jnp.where((bits > 0) & (index > first), index, units), axis=1, keepdims=True)
    unit = jnp.concatenate((first, second), axis=1)
    mask = jnp.sum(jnp.where(unit[:, :, None] == index, bits[:, None, :], 0), axis=2)
    return jnp.where(unit == units, -1, unit), mask, local


def unit_place(unit, blocks):
    head = unit // blocks
    return (
        pl.ds(pl.multiple_of((unit - head * blocks) * BLOCK, BLOCK), BLOCK),
        pl.ds(pl.multiple_of(head * HD, HD), HD),
    )


def pack_kernel(blocks, asked, keys, values, out):
    def body(slot, _):
        @pl.when(asked[slot] >= 0)
        def _():
            rows, cols = unit_place(asked[slot], blocks)
            out[slot, :, :HD] = keys[rows, cols]
            out[slot, :, HD:] = values[rows, cols]

        return 0

    lax.fori_loop(0, out.shape[0], body, 0)


def backward(key, value, query, grad, log_row, delta_row, allowed=None):
    scale = HD**-0.5
    probs = jnp.exp(dot(key, query, NT) * scale - log_row)
    if allowed is not None:
        probs = jnp.where(allowed, probs, 0.0)
    dscores = (probs * (dot(value, grad, NT) - delta_row)).astype(jnp.bfloat16)
    return dot(key, dscores, TN), dot(dscores, query) * scale, dot(probs.astype(jnp.bfloat16), grad)


def attend_kernel(
    unit, mask, local, queries, keys, values, grads, logs, deltas, pulled, back, dqt, dk, dv, total
):
    heads = logs.shape[0]
    tokens = queries.shape[0]
    blocks = tokens // BLOCK
    lane_block = lax.broadcasted_iota(jnp.int32, (1, tokens), 1) // BLOCK

    def open_logs(head, bits):
        return jnp.where(((bits >> lane_block) & 1) == 1, logs[head], FAR)

    def one_head(head, _):
        cols = pl.ds(pl.multiple_of(head * HD, HD), HD)
        query, grad = queries[:, cols], grads[:, cols]
        rows = lax.broadcasted_iota(jnp.int32, (BLOCK, tokens), 0)
        lanes = lax.broadcasted_iota(jnp.int32, (BLOCK, tokens), 1)
        sums = jnp.zeros((HD, tokens), jnp.float32)
        for block in range(blocks):
            place = slice(block * BLOCK, (block + 1) * BLOCK)
            dq, dk_part, dv_part = backward(
                keys[place, cols],
                values[place, cols],
                query,
                grad,
                open_logs(head, local[head * blocks + block]),
                deltas[head],
                rows + block * BLOCK <= lanes,
            )
            sums += dq
            dk[place, cols] = dk_part
            dv[place, cols] = dv_part
        total[head] = sums
        return 0

    lax.fori_loop(0, heads, one_head, 0)

    def one_slot(slot, _):
        @pl.when(unit[slot] >= 0)
        def _():
            head = unit[slot] // blocks
            cols = pl.ds(pl.multiple_of(head * HD, HD), HD)
            dq, dk_part, dv_part = backward(
                pulled[slot, :, :HD],
                pulled[slot, :, HD:],
                queries[:, cols],
                grads[:, cols],
                open_logs(head, mask[slot]),
                deltas[head],
            )
            total[head] += dq
            back[slot, :, :HD] = dk_part.astype(jnp.bfloat16)
            back[slot, :, HD:] = dv_part.astype(jnp.bfloat16)

        return 0

    lax.fori_loop(0, pulled.shape[0], one_slot, 0)
    dqt[...] = (total[...] * HD**-0.5).astype(jnp.bfloat16)


def settle_kernel(blocks, asked, returned, dk, dv, dk_out, dv_out, dk_sum, dv_sum):
    dk_sum[...] = dk[...]
    dv_sum[...] = dv[...]

    def body(slot, _):
        @pl.when(asked[slot] >= 0)
        def _():
            rows, cols = unit_place(asked[slot], blocks)
            dk_sum[rows, cols] += returned[slot, :, :HD].astype(jnp.float32)
            dv_sum[rows, cols] += returned[slot, :, HD:].astype(jnp.float32)

        return 0

    lax.fori_loop(0, returned.shape[0], body, 0)
    dk_out[...] = dk_sum[...].astype(jnp.bfloat16)
    dv_out[...] = dv_sum[...].astype(jnp.bfloat16)


SMEM = pl.BlockSpec(memory_space=pltpu.SMEM)
VMEM = pl.BlockSpec(memory_space=pltpu.VMEM)
LIMIT = pltpu.CompilerParams(vmem_limit_bytes=48 * 2**20)


def per_device(queries, keys, values, outputs, out_grad, log_sum, selected, w_query):
    tokens, width = queries.shape
    heads, blocks, _ = selected.shape
    shards = lax.axis_size("seq")
    me = lax.axis_index("seq")
    slots = shards * CAP
    low = jax.ShapeDtypeStruct((slots, BLOCK, 2 * HD), jnp.bfloat16)
    unit, mask, local = request_tables(selected, me, shards)
    asked = lax.all_to_all(unit, "seq", split_axis=0, concat_axis=0, tiled=True).reshape(-1)
    outgoing = pl.pallas_call(
        functools.partial(pack_kernel, blocks),
        out_shape=low,
        in_specs=[SMEM, VMEM, VMEM],
        out_specs=VMEM,
        compiler_params=LIMIT,
        name="pack",
    )(asked, keys, values)
    pulled = lax.all_to_all(
        outgoing.reshape(shards, CAP, BLOCK, 2 * HD), "seq", split_axis=0, concat_axis=0, tiled=True
    ).reshape(slots, BLOCK, 2 * HD)
    products = out_grad.astype(jnp.float32) * outputs.astype(jnp.float32)
    delta = jnp.sum(products.reshape(tokens, heads, HD), axis=-1).T
    wide = jax.ShapeDtypeStruct((tokens, width), jnp.float32)
    back, dqt, dk, dv = pl.pallas_call(
        attend_kernel,
        out_shape=(low, jax.ShapeDtypeStruct((heads, HD, tokens), jnp.bfloat16), wide, wide),
        in_specs=[SMEM] * 3 + [VMEM] * 7,
        out_specs=(VMEM,) * 4,
        scratch_shapes=[pltpu.VMEM((heads, HD, tokens), jnp.float32)],
        compiler_params=LIMIT,
        name="attend",
    )(
        unit.reshape(-1),
        mask.reshape(-1),
        local,
        queries,
        keys,
        values,
        out_grad,
        log_sum[:, None, :],
        delta[:, None, :],
        pulled,
    )
    returned = lax.all_to_all(
        back.reshape(shards, CAP, BLOCK, 2 * HD), "seq", split_axis=0, concat_axis=0, tiled=True
    ).reshape(slots, BLOCK, 2 * HD)
    result = jax.ShapeDtypeStruct((tokens, width), jnp.bfloat16)
    key_gradient, value_gradient = pl.pallas_call(
        functools.partial(settle_kernel, blocks),
        out_shape=(result, result),
        in_specs=[SMEM] + [VMEM] * 3,
        out_specs=(VMEM, VMEM),
        scratch_shapes=[pltpu.VMEM((tokens, width), jnp.float32)] * 2,
        compiler_params=LIMIT,
        name="settle",
    )(asked, returned, dk, dv)
    x_grad = lax.psum_scatter(
        dot(dqt.reshape(width, tokens), w_query, (((0,), (1,)), ((), ()))),
        "head",
        scatter_dimension=0,
        tiled=True,
    ).astype(jnp.bfloat16)
    return x_grad, key_gradient, value_gradient


def solution(mesh):
    in_specs = (P("seq", "head"),) * 5 + (P("head", "seq"), P("head", "seq", None), P(None, "head"))
    out_specs = (P(("seq", "head"), None), P("seq", "head"), P("seq", "head"))
    return jax.shard_map(
        per_device, mesh=mesh, in_specs=in_specs, out_specs=out_specs, check_vma=False
    )
```

profile of v0, /device:TPU:34, one launch (start us, length us, event | category | flops | bytes accessed | tf_op | source)
XLA Modules:
  0.0 322.7 jit_solution(7821171764726501931)
XLA Ops:
  7.2 0.9 fusion
  8.1 0.1 select_reduce_fusion.4
  8.2 0.1 copy.27
  8.4 1.4 select_reduce_fusion.2
  9.7 1.3 select_reduce_fusion.1
  11.1 0.1 copy.33
  11.2 19.1 %all_to_all.16 = s32[64,1,2]{2,1,0:T(1,128)S(1)} all-to-all(s32[64,1,2]{2,1,0:T(1,128)S(1)} %copy.33), channel_id=1, replica_groups=mesh['seq'=64,'head'=4] {'seq'}, dimensions={0} | all-to-all | bytes 1024 | tf_op jit(solution)/shard_map/all_to_all | solution.py:162
  30.2 0.5 broadcast.86
  30.8 0.7 reduce.6
  31.5 0.1 reshape.167.asked
  31.6 0.0 copy-start.2
  31.6 1.0 copy-done.2
  32.7 1.0 copy-done.4
  33.7 4.1 %pack.1 = bf16[128,64,256]{2,1,0:T(8,128)(2,1)S(1)} custom-call(s32[128]{0:T(128)S(1)} %reshape.167.asked, bf16[256,1024]{1,0:T(8,128)(2,1)S(1)} %copy-done.2, bf16[256,1024]{1,0:T(8,128)(2,1)S(1)} %copy-done.4), custom_call_target="tpu_custom_call" | custom-call | tf_op jit(solution)/shard_map/pack/pallas_call | solution.py:163
  37.8 0.0 copy-start
  37.8 1.9 copy-done
  39.7 7.7 %all-to-all-start.1 = ((bf16[64,2,64,256]{3,2,1,0:T(8,128)(2,1)}), bf16[64,2,64,256]{3,2,1,0:T(8,128)(2,1)}, u32[]{:S(2)}, u32[]{:S(2)}) async-start(bf16[64,2,64,256]{3,2,1,0:T(8,128)(2,1)} %bitcast.19), calls=%async_computation.1 | async-start | bytes 8388608 | tf_op jit(solution)/shard_map/all_to_all | solution.py:171
  47.5 0.0 copy-start.3
  47.5 0.0 copy-start.5
  47.5 0.0 copy-start.8
  47.5 0.0 reduce-scatter.2.cloned.1.call-start
  47.5 0.1 copy.29
  47.6 0.0 copy-done.10
  47.7 0.1 copy.31
  47.7 0.1 reduce_sum.41.local
  47.8 0.1 copy.28
  47.9 0.1 concatenate.25
  48.1 0.1 copy.30
  48.2 0.1 reshape.165.mask
  48.4 0.0 copy-done.1
  48.4 0.0 copy-done.9
  48.4 0.2 multiply_bitcast_fusion
  48.5 0.2 copy.35
  48.8 0.3 reduce_sum.42
  49.1 0.1 copy.32
  49.2 93.6 %all-to-all-done.1 = bf16[64,2,64,256]{3,2,1,0:T(8,128)(2,1)} async-done(((bf16[64,2,64,256]{3,2,1,0:T(8,128)(2,1)}), bf16[64,2,64,256]{3,2,1,0:T(8,128)(2,1)}, u32[]{:S(2)}, u32[]{:S(2)}) %all-to-all-start.1) | async-done | bytes 4194336 | tf_op jit(solution)/shard_map/all_to_all | solution.py:171
  142.8 0.0 copy-done.3
  142.8 0.0 copy-done.5
  142.8 0.0 copy-done.8
  142.8 18.8 %attend.1 = (bf16[128,64,256]{2,1,0:T(8,128)(2,1)}, bf16[8,128,256]{2,1,0:T(8,128)(2,1)S(1)}, f32[256,1024]{1,0:T(8,128)S(1)}, f32[256,1024]{1,0:T(8,128)S(1)}) custom-call(s32[128]{0:T(128)S(1)} %compare_select_fusion.1.unit, s32[128]{0:T(128)S(1)} %reshape.165.mask, s32[32]{0:T(128)S(1)} %reduce_sum.41.local, bf16[256,1024]{1,0:T(8,128)(2,1)S(1)} %copy-done.8, ...), custom_call_target="tpu_custom_call" | custom-call | tf_op jit(solution)/shard_map/attend/pallas_call | solution.py:177
  161.6 1.0 copy-done.6
  162.5 7.8 %fusion.1 = f32[256,4096]{1,0:T(8,128)} fusion(bf16[1024,256]{1,0:T(8,128)(2,1)S(1)} %bitcast.20, bf16[4096,1024]{1,0:T(8,128)(2,1)} %param.15), kind=kOutput, calls=%fused_computation.17 | convolution fusion | flops 2147483648 | bytes 13107200 | tf_op jit(solution)/shard_map/dot_general | solution.py:20
  170.3 0.0 reduce-scatter.2.cloned.1.call-update
  170.3 0.0 copy-start.7
  170.3 136.4 %all_to_all.17 = bf16[64,2,64,256]{3,2,1,0:T(8,128)(2,1)} all-to-all(bf16[64,2,64,256]{3,2,1,0:T(8,128)(2,1)} %bitcast.22), channel_id=1, replica_groups=mesh['seq'=64,'head'=4] {'seq'}, dimensions={0} | all-to-all | bytes 8388608 | tf_op jit(solution)/shard_map/all_to_all | solution.py:197
  306.8 0.0 copy-done.7
  306.8 7.1 %settle.1 = (bf16[256,1024]{1,0:T(8,128)(2,1)}, bf16[256,1024]{1,0:T(8,128)(2,1)}) custom-call(s32[128]{0:T(128)S(1)} %reshape.167.asked, bf16[128,64,256]{2,1,0:T(8,128)(2,1)} %bitcast.21, f32[256,1024]{1,0:T(8,128)S(1)} %get-tuple-element.11.dk, f32[256,1024]{1,0:T(8,128)S(1)} %copy-done.7), custom_call_target="tpu_custom_call" | custom-call | tf_op jit(solution)/shard_map/settle/pallas_call | solution.py:201
  313.8 2.1 convert_element_type.11
  (16 shorter events, 0.1 us)
Async XLA Ops:
  31.6 1.0 copy-start.2
  32.7 1.0 copy-start.4
  37.8 1.9 copy-start
  39.7 7.9 %copy-start.10 = (f32[8,256]{1,0:T(8,128)S(1)}, f32[8,256]{1,0:T(8,128)}, u32[]{:S(2)}) copy-start(f32[8,256]{1,0:T(8,128)} %param.13) | copy-start | bytes 24580
  39.7 8.6 %copy-start.1 = (bf16[256,1024]{1,0:T(8,128)(2,1)S(1)}, bf16[256,1024]{1,0:T(8,128)(2,1)}, u32[]{:S(2)}) copy-start(bf16[256,1024]{1,0:T(8,128)(2,1)} %grads.1) | copy-start | bytes 1572868
  39.7 8.6 %copy-start.9 = (bf16[256,1024]{1,0:T(8,128)(2,1)S(1)}, bf16[256,1024]{1,0:T(8,128)(2,1)}, u32[]{:S(2)}) copy-start(bf16[256,1024]{1,0:T(8,128)(2,1)} %param.11) | copy-start | bytes 1572868
  39.7 103.1 %all-to-all-start.1 = ((bf16[64,2,64,256]{3,2,1,0:T(8,128)(2,1)}), bf16[64,2,64,256]{3,2,1,0:T(8,128)(2,1)}, u32[]{:S(2)}, u32[]{:S(2)}) async-start(bf16[64,2,64,256]{3,2,1,0:T(8,128)(2,1)} %bitcast.19), calls=%async_computation.1 | async-start | bytes 8388608 | tf_op jit(solution)/shard_map/all_to_all | solution.py:171
  47.5 95.3 %copy-start.3 = (bf16[256,1024]{1,0:T(8,128)(2,1)S(1)}, bf16[256,1024]{1,0:T(8,128)(2,1)}, u32[]{:S(2)}) copy-start(bf16[256,1024]{1,0:T(8,128)(2,1)} %keys.3) | copy-start | bytes 1572868
  47.5 95.3 %copy-start.5 = (bf16[256,1024]{1,0:T(8,128)(2,1)S(1)}, bf16[256,1024]{1,0:T(8,128)(2,1)}, u32[]{:S(2)}) copy-start(bf16[256,1024]{1,0:T(8,128)(2,1)} %values.3) | copy-start | bytes 1572868
  47.5 95.3 %copy-start.8 = (bf16[256,1024]{1,0:T(8,128)(2,1)S(1)}, bf16[256,1024]{1,0:T(8,128)(2,1)}, u32[]{:S(2)}) copy-start(bf16[256,1024]{1,0:T(8,128)(2,1)} %queries.1) | copy-start | bytes 1572868
  47.5 266.3 %reduce-scatter.2.cloned.1.call-start = ((), (), s32[]{:S(2)}) async-start(), calls=%async_computation.4 | async-start | bytes 5242880 | tf_op jit(solution)/shard_map/reduce_scatter | solution.py:210
  161.6 1.0 copy-start.6
  170.3 136.4 %copy-start.7 = (f32[256,1024]{1,0:T(8,128)S(1)}, f32[256,1024]{1,0:T(8,128)}, u32[]{:S(2)}) copy-start(f32[256,1024]{1,0:T(8,128)} %copy-done.6) | copy-start | bytes 3145732
Sparse Core Ops, SparseCore 0:
  170.5 81.1 reduce-scatter.1
where the time goes:
time: 325 us; the launch traced here: 323 us
  blocking collectives  155 us (48%)
  waiting for transfers between devices  93.6 us (29%)
  Pallas kernels  29.9 us (9%)
  between operations  14.2 us (4%)
  matrix products  7.78 us (2%)
  starting transfers between devices  7.76 us (2%)
  other arithmetic  7.08 us (2%)
  local copies, waits for them, and re-layouts  6.88 us (2%)
    all_to_all x1, blocking collectives, per_device(): lax.all_to_all(back.reshape(shards, CAP, BLOCK, 2 * HD), 'seq', split_axi...  136 us
    all_to_all x1, waiting for transfers between devices, per_device(): lax.all_to_all(outgoing.reshape(shards, CAP, BLOCK, 2 * HD), 'seq', split...  93.6 us
    all_to_all x1, blocking collectives, per_device(): lax.all_to_all(unit, 'seq', split_axis=0, concat_axis=0, tiled=True)  19.1 us
    pallas_call x1, Pallas kernels, per_device(): pl.pallas_call(attend_kernel, out_shape=(low, jax.ShapeDtypeStruct((heads...  18.8 us
    dot_general x1, matrix products, dot(): return lax.dot_general(a, b, dims, preferred_element_type=jnp.float32)  7.78 us
    all_to_all x1, starting transfers between devices, per_device(): lax.all_to_all(outgoing.reshape(shards, CAP, BLOCK, 2 * HD), 'seq', split...  7.72 us
    pallas_call x1, Pallas kernels, per_device(): pl.pallas_call(functools.partial(settle_kernel, blocks), out_shape=(resul...  7.06 us
  transfers between devices with their start and end apart: 2, of which 1 were waited for; matrix products, arithmetic and copies ran while one was open for 0% of the time, Pallas kernels for 2%

commit v1 on v0

--- a/solution.py
+++ b/solution.py
@@ -55,6 +55,10 @@
             out[slot, :, :HD] = keys[rows, cols]
             out[slot, :, HD:] = values[rows, cols]
 
+        @pl.when(asked[slot] < 0)
+        def _():
+            out[slot] = jnp.zeros(out.shape[1:], out.dtype)
+
         return 0
 
     lax.fori_loop(0, out.shape[0], body, 0)
@@ -69,20 +73,88 @@
     return dot(key, dscores, TN), dot(dscores, query) * scale, dot(probs.astype(jnp.bfloat16), grad)
 
 
-def attend_kernel(
-    unit, mask, local, queries, keys, values, grads, logs, deltas, pulled, back, dqt, dk, dv, total
+def exchange_kernel(
+    picked,
+    mask,
+    local,
+    queries,
+    keys,
+    values,
+    grads,
+    logs,
+    deltas,
+    outgoing,
+    dqt,
+    dk,
+    dv,
+    returned,
+    pulled,
+    back,
+    total,
+    query_heads,
+    grad_heads,
+    pull_send,
+    pull_recv,
+    back_send,
+    back_recv,
 ):
+    me = lax.axis_index("seq")
+    shards = outgoing.shape[0]
     heads = logs.shape[0]
     tokens = queries.shape[0]
     blocks = tokens // BLOCK
     lane_block = lax.broadcasted_iota(jnp.int32, (1, tokens), 1) // BLOCK
 
+    def pull_copy(slot_from, slot_to, target, index):
+        return pltpu.make_async_remote_copy(
+            src_ref=outgoing.at[slot_from],
+            dst_ref=pulled.at[slot_to],
+            send_sem=pull_send.at[slot_from],
+            recv_sem=pull_recv.at[index],
+            device_id={"seq": target},
+            device_id_type=pl.DeviceIdType.MESH,
+        )
+
+    def back_copy(slot_from, slot_to, target, index):
+        return pltpu.make_async_remote_copy(
+            src_ref=back.at[slot_from],
+            dst_ref=returned.at[slot_to],
+            send_sem=back_send.at[slot_from],
+            recv_sem=back_recv.at[index],
+            device_id={"seq": target},
+            device_id_type=pl.DeviceIdType.MESH,
+        )
+
+    barrier = pltpu.get_barrier_semaphore()
+
+    def greet(step, _):
+        pl.semaphore_signal(
+            barrier,
+            inc=1,
+            device_id={"seq": lax.rem(me + step, shards)},
+            device_id_type=pl.DeviceIdType.MESH,
+        )
+        return 0
+
+    lax.fori_loop(1, shards, greet, 0)
+    pl.semaphore_wait(barrier, shards - 1)
+
+    def send(target, _):
+        pull_copy(target, me, target, me).start()
+        return 0
+
+    lax.fori_loop(me + 1, shards, send, 0)
+    for head in range(heads):
+        cols = slice(head * HD, (head + 1) * HD)
+        query_heads[head] = queries[:, cols]
+        grad_heads[head] = grads[:, cols]
+
     def open_logs(head, bits):
         return jnp.where(((bits >> lane_block) & 1) == 1, logs[head], FAR)
 
     def one_head(head, _):
         cols = pl.ds(pl.multiple_of(head * HD, HD), HD)
-        query, grad = queries[:, cols], grads[:, cols]
+        query, grad = query_heads[head], grad_heads[head]
         rows = lax.broadcasted_iota(jnp.int32, (BLOCK, tokens), 0)
         lanes = lax.broadcasted_iota(jnp.int32, (BLOCK, tokens), 1)
         sums = jnp.zeros((HD, tokens), jnp.float32)
@@ -105,27 +177,45 @@
 
     lax.fori_loop(0, heads, one_head, 0)
 
-    def one_slot(slot, _):
-        @pl.when(unit[slot] >= 0)
-        def _():
-            head = unit[slot] // blocks
-            cols = pl.ds(pl.multiple_of(head * HD, HD), HD)
+    def one_source(step, _):
+        source = me - step
+        pull_copy(source, source, source, source).wait_recv()
+        parts = []
+        for slot in range(CAP):
+            head = picked[source * CAP + slot]
             dq, dk_part, dv_part = backward(
-                pulled[slot, :, :HD],
-                pulled[slot, :, HD:],
-                queries[:, cols],
-                grads[:, cols],
-                open_logs(head, mask[slot]),
+                pulled[source, slot, :, :HD],
+                pulled[source, slot, :, HD:],
+                query_heads[head],
+                grad_heads[head],
+                open_logs(head, mask[source * CAP + slot]),
                 deltas[head],
             )
-            total[head] += dq
-            back[slot, :, :HD] = dk_part.astype(jnp.bfloat16)
-            back[slot, :, HD:] = dv_part.astype(jnp.bfloat16)
-
-        return 0
-
-    lax.fori_loop(0, pulled.shape[0], one_slot, 0)
+            back[source, slot, :, :HD] = dk_part.astype(jnp.bfloat16)
+            back[source, slot, :, HD:] = dv_part.astype(jnp.bfloat16)
+            parts.append((head, dq))
+        back_copy(source, me, source, me).start()
+        for head in range(heads):
+            total[head] += sum(
+                jnp.where(jnp.full(dq.shape, at, jnp.int32) == head, dq, 0.0) for at, dq in parts
+            )
+        return 0
+
+    lax.fori_loop(1, me + 1, one_source, 0)
     dqt[...] = (total[...] * HD**-0.5).astype(jnp.bfloat16)
+
+    def finish_owner(target, _):
+        pull_copy(target, target, target, target).wait_send()
+        back_copy(target, target, target, target).wait_recv()
+        return 0
+
+    lax.fori_loop(me + 1, shards, finish_owner, 0)
+
+    def finish_requester(source, _):
+        back_copy(source, source, source, source).wait_send()
+        return 0
+
+    lax.fori_loop(0, me, finish_requester, 0)
 
 
 def settle_kernel(blocks, asked, returned, dk, dv, dk_out, dv_out, dk_sum, dv_sum):
@@ -168,22 +258,34 @@
         compiler_params=LIMIT,
         name="pack",
     )(asked, keys, values)
-    pulled = lax.all_to_all(
-        outgoing.reshape(shards, CAP, BLOCK, 2 * HD), "seq", split_axis=0, concat_axis=0, tiled=True
-    ).reshape(slots, BLOCK, 2 * HD)
     products = out_grad.astype(jnp.float32) * outputs.astype(jnp.float32)
     delta = jnp.sum(products.reshape(tokens, heads, HD), axis=-1).T
     wide = jax.ShapeDtypeStruct((tokens, width), jnp.float32)
-    back, dqt, dk, dv = pl.pallas_call(
-        attend_kernel,
-        out_shape=(low, jax.ShapeDtypeStruct((heads, HD, tokens), jnp.bfloat16), wide, wide),
+    paired = (shards, CAP, BLOCK, 2 * HD)
+    dqt, dk, dv, returned = pl.pallas_call(
+        exchange_kernel,
+        out_shape=(
+            jax.ShapeDtypeStruct((heads, HD, tokens), jnp.bfloat16),
+            wide,
+            wide,
+            jax.ShapeDtypeStruct(paired, jnp.bfloat16),
+        ),
         in_specs=[SMEM] * 3 + [VMEM] * 7,
         out_specs=(VMEM,) * 4,
-        scratch_shapes=[pltpu.VMEM((heads, HD, tokens), jnp.float32)],
-        compiler_params=LIMIT,
-        name="attend",
+        scratch_shapes=[
+            pltpu.VMEM(paired, jnp.bfloat16),
+            pltpu.VMEM(paired, jnp.bfloat16),
+            pltpu.VMEM((heads, HD, tokens), jnp.float32),
+            pltpu.VMEM((heads, tokens, HD), jnp.bfloat16),
+            pltpu.VMEM((heads, tokens, HD), jnp.bfloat16),
+        ]
+        + [pltpu.SemaphoreType.DMA((shards,))] * 4,
+        compiler_params=pltpu.CompilerParams(
+            vmem_limit_bytes=48 * 2**20, collective_id=0, has_side_effects=True
+        ),
+        name="exchange",
     )(
-        unit.reshape(-1),
+        jnp.maximum(unit.reshape(-1), 0) // blocks,
         mask.reshape(-1),
         local,
         queries,
@@ -192,11 +294,9 @@
         out_grad,
         log_sum[:, None, :],
         delta[:, None, :],
-        pulled,
+        outgoing.reshape(paired),
     )
-    returned = lax.all_to_all(
-        back.reshape(shards, CAP, BLOCK, 2 * HD), "seq", split_axis=0, concat_axis=0, tiled=True
-    ).reshape(slots, BLOCK, 2 * HD)
+    returned = returned.reshape(slots, BLOCK, 2 * HD)
     result = jax.ShapeDtypeStruct((tokens, width), jnp.bfloat16)
     key_gradient, value_gradient = pl.pallas_call(
         functools.partial(settle_kernel, blocks),

time: 325 us -> 288 us (0.89)
  blocking collectives: 155 us -> 0 us
  Pallas kernels: 29.9 us -> 172 us
  waiting for transfers between devices: 93.6 us -> 64.9 us
  starting transfers between devices: 7.76 us -> 11.6 us
  matrix products: 7.78 us -> 4.37 us
    all_to_all x2 -> x0, blocking collectives: 155 us -> none  [the longest x1 136 us: per_device(): lax.all_to_all(back.reshape(shards, CAP, BLOCK, 2 * HD), 'seq', split_axi...]
    pallas_call x1, Pallas kernels: 18.8 us -> 160 us  [per_device(): pl.pallas_call(exchange_kernel, out_shape=(jax.ShapeDtypeStruct((heads, H...]
    all_to_all x1, waiting for transfers between devices: 93.6 us -> 1.89 us  [per_device(): lax.all_to_all(unit, 'seq', split_axis=0, concat_axis=0, tiled=True)]
    reduce_scatter x1, waiting for transfers between devices: 0.01 us -> 63 us  [per_device(): lax.psum_scatter(dot(dqt.reshape(width, tokens), w_query, (((0,), (1,)),...]
    all_to_all x1, starting transfers between devices: 7.72 us -> 11.6 us  [per_device(): lax.all_to_all(unit, 'seq', split_axis=0, concat_axis=0, tiled=True)]
    dot_general x1, matrix products: 7.78 us -> 4.37 us  [dot(): return lax.dot_general(a, b, dims, preferred_element_type=jnp.float32)]
  transfers between devices with their start and end apart: 2 -> 2, of which waited for: 1 -> 2; matrix products, arithmetic and copies ran while one was open for 0% -> 2% of each run, Pallas kernels for 2% -> 2%
where the time goes in v1:
time: 288 us; the launch traced here: 286 us
  Pallas kernels  172 us (60%)
  waiting for transfers between devices  64.9 us (23%)
  between operations  14.2 us (5%)
  starting transfers between devices  11.6 us (4%)
  other arithmetic  9.65 us (3%)
  local copies, waits for them, and re-layouts  9.2 us (3%)
  matrix products  4.37 us (2%)
    pallas_call x1, Pallas kernels, per_device(): pl.pallas_call(exchange_kernel, out_shape=(jax.ShapeDtypeStruct((heads, H...  160 us
    reduce_scatter x1, waiting for transfers between devices, per_device(): lax.psum_scatter(dot(dqt.reshape(width, tokens), w_query, (((0,), (1,)),...  63 us
    all_to_all x1, starting transfers between devices, per_device(): lax.all_to_all(unit, 'seq', split_axis=0, concat_axis=0, tiled=True)  11.6 us
    pallas_call x1, Pallas kernels, per_device(): pl.pallas_call(functools.partial(settle_kernel, blocks), out_shape=(resul...  6.92 us
    unnamed x21, local copies, waits for them, and re-layouts  6.23 us
  transfers between devices with their start and end apart: 2, of which 2 were waited for; matrix products, arithmetic and copies ran while one was open for 2% of the time, Pallas kernels for 2%

profile of v1, /device:TPU:34, one launch (start us, length us, event | category | flops | bytes accessed | tf_op | source)
XLA Modules:
  0.0 285.8 jit_solution(1233579324823109708)
XLA Ops:
  7.2 0.0 copy-start.1
  7.2 0.0 copy-start.5
  7.2 0.0 copy-start.3
  7.2 0.0 copy-start.8
  7.3 1.0 fusion
  8.3 0.1 select_reduce_fusion.4
  8.4 0.1 copy.27
  8.5 1.4 select_reduce_fusion.2
  9.9 1.3 select_reduce_fusion.1
  11.2 0.7 copy.33
  12.0 11.6 %all-to-all-start = ((s32[64,1,2]{2,1,0:T(1,128)}), s32[64,1,2]{2,1,0:T(1,128)S(1)}, u32[]{:S(2)}, u32[]{:S(2)}) async-start(s32[64,1,2]{2,1,0:T(1,128)} %copy.33), calls=%async_computation | async-start | bytes 65536 | tf_op jit(solution)/shard_map/all_to_all | solution.py:252
  23.5 0.0 reduce-scatter.2.cloned.1.call-start
  23.6 0.1 copy.29
  23.7 0.1 copy.28
  23.8 0.1 concatenate.25
  23.9 1.4 multiply_bitcast_fusion
  25.4 0.7 broadcast_in_dim.132.logs
  26.1 0.1 copy.31
  26.1 0.1 reduce_sum.41.local
  26.2 0.1 copy.30
  26.3 0.1 reshape.159.mask
  26.5 1.2 copy.35
  27.6 1.6 reduce_sum.42
  29.2 0.1 copy.32
  29.3 1.9 all-to-all-done
  31.2 0.5 broadcast.93
  31.7 0.7 reduce.6
  32.4 0.1 reshape.161.asked
  32.6 0.0 copy-start.2
  32.6 1.0 copy-done.2
  33.6 1.0 copy-done.4
  34.7 5.0 %pack.1 = bf16[128,64,256]{2,1,0:T(8,128)(2,1)S(1)} custom-call(s32[128]{0:T(128)S(1)} %reshape.161.asked, bf16[256,1024]{1,0:T(8,128)(2,1)S(1)} %copy-done.2, bf16[256,1024]{1,0:T(8,128)(2,1)S(1)} %copy-done.4), custom_call_target="tpu_custom_call" | custom-call | tf_op jit(solution)/shard_map/pack/pallas_call | solution.py:253
  39.7 0.0 copy-start
  39.7 2.0 copy-done
  41.6 0.0 copy-done.1
  41.6 0.0 copy-done.5
  41.6 0.0 copy-done.3
  41.6 0.0 copy-done.8
  41.7 159.9 %exchange.1 = (bf16[8,128,256]{2,1,0:T(8,128)(2,1)S(1)}, f32[256,1024]{1,0:T(8,128)S(1)}, f32[256,1024]{1,0:T(8,128)S(1)}, bf16[64,2,64,256]{3,2,1,0:T(8,128)(2,1)}) custom-call(s32[128]{0:T(128)S(1)} %and_select_fusion.picked, s32[128]{0:T(128)S(1)} %reshape.159.mask, s32[32]{0:T(128)S(1)} %reduce_sum.41.local, bf16[256,1024]{1,0:T(8,128)(2,1)S(1)} %copy-done.8, ...), custom_call_target="tpu_custom_call" | custom-call | tf_op jit(solution)/shard_map/exchange/pallas_call | solution.py:265
  201.6 0.0 copy-start.6
  201.6 1.0 copy-done.6
  202.6 0.0 copy-done.9
  202.6 4.4 %fusion.2 = f32[256,4096]{1,0:T(8,128)} fusion(bf16[1024,256]{1,0:T(8,128)(2,1)S(1)} %bitcast.18, bf16[4096,1024]{1,0:T(8,128)(2,1)S(1)} %copy-done.9), kind=kOutput, calls=%fused_computation.19 | convolution fusion | flops 2147483648 | bytes 13107200 | tf_op jit(solution)/shard_map/dot_general | solution.py:20
  206.9 0.0 reduce-scatter.2.cloned.1.call-update
  206.9 0.0 copy-done.7
  207.0 6.9 %settle.1 = (bf16[256,1024]{1,0:T(8,128)(2,1)}, bf16[256,1024]{1,0:T(8,128)(2,1)}) custom-call(s32[128]{0:T(128)S(1)} %reshape.161.asked, bf16[128,64,256]{2,1,0:T(8,128)(2,1)} %bitcast.19, f32[256,1024]{1,0:T(8,128)S(1)} %get-tuple-element.11.dk, f32[256,1024]{1,0:T(8,128)S(1)} %copy-done.7), custom_call_target="tpu_custom_call" | custom-call | tf_op jit(solution)/shard_map/settle/pallas_call | solution.py:301
  213.9 63.0 %reduce-scatter.2.cloned.1.call-done = f32[64,4096]{1,0:T(8,128)} async-done(((f32[256,4096]{1,0:T(8,128)}), f32[64,4096]{1,0:T(8,128)}) %reduce-scatter.2.cloned.1.call-update) | async-done | bytes 1048592 | tf_op jit(solution)/shard_map/reduce_scatter | solution.py:310
  276.8 2.1 convert_element_type.11
  (12 shorter events, 0.1 us)
Async XLA Ops:
  7.2 34.5 %copy-start.1 = (bf16[256,1024]{1,0:T(8,128)(2,1)S(1)}, bf16[256,1024]{1,0:T(8,128)(2,1)}, u32[]{:S(2)}) copy-start(bf16[256,1024]{1,0:T(8,128)(2,1)} %grads.1) | copy-start | bytes 1572868
  7.2 34.5 %copy-start.5 = (bf16[256,1024]{1,0:T(8,128)(2,1)S(1)}, bf16[256,1024]{1,0:T(8,128)(2,1)}, u32[]{:S(2)}) copy-start(bf16[256,1024]{1,0:T(8,128)(2,1)} %values.3) | copy-start | bytes 1572868
  7.2 34.5 %copy-start.3 = (bf16[256,1024]{1,0:T(8,128)(2,1)S(1)}, bf16[256,1024]{1,0:T(8,128)(2,1)}, u32[]{:S(2)}) copy-start(bf16[256,1024]{1,0:T(8,128)(2,1)} %keys.3) | copy-start | bytes 1572868
  7.2 34.4 %copy-start.8 = (bf16[256,1024]{1,0:T(8,128)(2,1)S(1)}, bf16[256,1024]{1,0:T(8,128)(2,1)}, u32[]{:S(2)}) copy-start(bf16[256,1024]{1,0:T(8,128)(2,1)} %queries.1) | copy-start | bytes 1572868
  12.0 19.2 %all-to-all-start = ((s32[64,1,2]{2,1,0:T(1,128)}), s32[64,1,2]{2,1,0:T(1,128)S(1)}, u32[]{:S(2)}, u32[]{:S(2)}) async-start(s32[64,1,2]{2,1,0:T(1,128)} %copy.33), calls=%async_computation | async-start | bytes 65536 | tf_op jit(solution)/shard_map/all_to_all | solution.py:252
  23.5 253.3 %reduce-scatter.2.cloned.1.call-start = ((), (), s32[]{:S(2)}) async-start(), calls=%async_computation.2 | async-start | bytes 5242880 | tf_op jit(solution)/shard_map/reduce_scatter | solution.py:310
  32.6 1.0 copy-start.2
  33.6 1.0 copy-start.4
  34.7 167.9 %copy-start.9 = (bf16[4096,1024]{1,0:T(8,128)(2,1)S(1)}, bf16[4096,1024]{1,0:T(8,128)(2,1)}, u32[]{:S(2)}) copy-start(bf16[4096,1024]{1,0:T(8,128)(2,1)} %param.15) | copy-start | bytes 25165828
  39.7 2.0 copy-start
  201.6 1.0 copy-start.6
  202.6 4.4 %copy-start.7 = (f32[256,1024]{1,0:T(8,128)S(1)}, f32[256,1024]{1,0:T(8,128)}, u32[]{:S(2)}) copy-start(f32[256,1024]{1,0:T(8,128)} %copy-done.6) | copy-start | bytes 3145732
Sparse Core Ops, SparseCore 0:
  207.1 69.7 reduce-scatter.1

commit v2 on v1

--- a/solution.py
+++ b/solution.py
@@ -47,23 +47,6 @@
     )
 
 
-def pack_kernel(blocks, asked, keys, values, out):
-    def body(slot, _):
-        @pl.when(asked[slot] >= 0)
-        def _():
-            rows, cols = unit_place(asked[slot], blocks)
-            out[slot, :, :HD] = keys[rows, cols]
-            out[slot, :, HD:] = values[rows, cols]
-
-        @pl.when(asked[slot] < 0)
-        def _():
-            out[slot] = jnp.zeros(out.shape[1:], out.dtype)
-
-        return 0
-
-    lax.fori_loop(0, out.shape[0], body, 0)
-
-
 def backward(key, value, query, grad, log_row, delta_row, allowed=None):
     scale = HD**-0.5
     probs = jnp.exp(dot(key, query, NT) * scale - log_row)
@@ -71,6 +54,10 @@
         probs = jnp.where(allowed, probs, 0.0)
     dscores = (probs * (dot(value, grad, NT) - delta_row)).astype(jnp.bfloat16)
     return dot(key, dscores, TN), dot(dscores, query) * scale, dot(probs.astype(jnp.bfloat16), grad)
+
+
+def offset_of(step, shards):
+    return lax.rem(step * 27, shards)
 
 
 def exchange_kernel(
@@ -83,23 +70,46 @@
     grads,
     logs,
     deltas,
-    outgoing,
-    dqt,
+    asking,
+    weight,
+    x_grad,
     dk,
     dv,
     returned,
+    asked,
+    outgoing,
+    units_here,
+    asked_here,
     pulled,
     back,
     total,
     query_heads,
     grad_heads,
+    weight_here,
+    dq_rows,
+    parts_out,
+    parts_in,
+    own_part,
     pull_send,
     pull_recv,
     back_send,
     back_recv,
+    part_send,
+    part_recv,
+    ask_send,
+    ask_recv,
+    weight_sem,
+    asked_sem,
 ):
     me = lax.axis_index("seq")
-    shards = outgoing.shape[0]
+    lane = lax.axis_index("head")
+    lanes_all = parts_out.shape[1]
+    stripe, piece = parts_out.shape[2:]
+    pieces = parts_out.shape[0]
+    weight_copy = pltpu.make_async_copy(weight, weight_here, weight_sem)
+    weight_copy.start()
+    asked[...] = jnp.full(asked.shape, -1, jnp.int32)
+    shards = asking.shape[0]
     heads = logs.shape[0]
     tokens = queries.shape[0]
     blocks = tokens // BLOCK
@@ -125,6 +135,26 @@
             device_id_type=pl.DeviceIdType.MESH,
         )
 
+    def ask_copy(slot_from, slot_to, target, index):
+        return pltpu.make_async_remote_copy(
+            src_ref=asking.at[slot_from],
+            dst_ref=asked.at[slot_to],
+            send_sem=ask_send.at[slot_from],
+            recv_sem=ask_recv.at[index],
+            device_id={"seq": target},
+            device_id_type=pl.DeviceIdType.MESH,
+        )
+
+    def part_copy(at, slot_from, slot_to, target, index):
+        return pltpu.make_async_remote_copy(
+            src_ref=parts_out.at[at, slot_from],
+            dst_ref=parts_in.at[at, slot_to],
+            send_sem=part_send.at[at, slot_from],
+            recv_sem=part_recv.at[at, index],
+            device_id={"head": target},
+            device_id_type=pl.DeviceIdType.MESH,
+        )
+
     barrier = pltpu.get_barrier_semaphore()
 
     def greet(step, _):
@@ -137,17 +167,57 @@
         return 0
 
     lax.fori_loop(1, shards, greet, 0)
-    pl.semaphore_wait(barrier, shards - 1)
-
-    def send(target, _):
-        pull_copy(target, me, target, me).start()
-        return 0
-
-    lax.fori_loop(me + 1, shards, send, 0)
+    for step in range(1, lanes_all):
+        pl.semaphore_signal(
+            barrier,
+            inc=1,
+            device_id={"head": lax.rem(lane + step, lanes_all)},
+            device_id_type=pl.DeviceIdType.MESH,
+        )
+    pl.semaphore_wait(barrier, shards - 1 + lanes_all - 1)
+
+    def ask(source, _):
+        ask_copy(source, me, source, me).start()
+        return 0
+
+    lax.fori_loop(0, me, ask, 0)
     for head in range(heads):
         cols = slice(head * HD, (head + 1) * HD)
         query_heads[head] = queries[:, cols]
         grad_heads[head] = grads[:, cols]
+        for block in range(blocks):
+            rows = slice(block * BLOCK, (block + 1) * BLOCK)
+            units_here[head * blocks + block, :, :HD] = keys[rows, cols]
+            units_here[head * blocks + block, :, HD:] = values[rows, cols]
+
+    def heard(target, _):
+        ask_copy(target, target, target, target).wait_recv()
+        return 0
+
+    lax.fori_loop(me + 1, shards, heard, 0)
+    asked_copy = pltpu.make_async_copy(asked, asked_here, asked_sem)
+    asked_copy.start()
+    asked_copy.wait()
+
+    def send(target):
+        for slot in range(CAP):
+            wanted = asked_here[target, 0, slot]
+            found = units_here[jnp.maximum(wanted, 0)]
+            outgoing[target, slot] = jnp.where(
+                jnp.full(found.shape, wanted, jnp.int32) >= 0, found, jnp.zeros_like(found)
+            )
+        pull_copy(target, me, target, me).start()
+
+    def send_step(step, _):
+        target = me + offset_of(step, shards)
+
+        @pl.when(target < shards)
+        def _():
+            send(target)
+
+        return 0
+
+    lax.fori_loop(1, shards, send_step, 0)
 
     def open_logs(head, bits):
         return jnp.where(((bits >> lane_block) & 1) == 1, logs[head], FAR)
@@ -201,8 +271,43 @@
             )
         return 0
 
-    lax.fori_loop(1, me + 1, one_source, 0)
-    dqt[...] = (total[...] * HD**-0.5).astype(jnp.bfloat16)
+    def source_step(step, _):
+        offset = offset_of(step, shards)
+
+        @pl.when(offset <= me)
+        def _():
+            one_source(offset, 0)
+
+        return 0
+
+    lax.fori_loop(1, shards, source_step, 0)
+    for head in range(heads):
+        dq_rows[:, head * HD : (head + 1) * HD] = (total[head] * HD**-0.5).T.astype(jnp.bfloat16)
+    weight_copy.wait()
+
+    def one_piece(at, _):
+        columns = pl.ds(pl.multiple_of(at * piece, piece), piece)
+        product = dot(dq_rows[...], weight_here[columns, :], NT).reshape(lanes_all, stripe, piece)
+        own_part[at] = product
+        parts_out[at] = product.astype(jnp.bfloat16)
+        for step in range(1, lanes_all):
+            target = lax.rem(lane + step, lanes_all)
+            part_copy(at, target, lane, target, lane).start()
+        return 0
+
+    lax.fori_loop(0, pieces, one_piece, 0)
+
+    def one_sum(at, _):
+        row_sum = own_part[at, lane]
+        for step in range(1, lanes_all):
+            source = lax.rem(lane + step, lanes_all)
+            part_copy(at, source, source, source, source).wait()
+            row_sum += parts_in[at, source].astype(jnp.float32)
+        columns = pl.ds(pl.multiple_of(at * piece, piece), piece)
+        x_grad[:, columns] = row_sum.astype(jnp.bfloat16)
+        return 0
+
+    lax.fori_loop(0, pieces, one_sum, 0)
 
     def finish_owner(target, _):
         pull_copy(target, target, target, target).wait_send()
@@ -213,6 +318,7 @@
 
     def finish_requester(source, _):
         back_copy(source, source, source, source).wait_send()
+        ask_copy(source, source, source, source).wait_send()
         return 0
 
     lax.fori_loop(0, me, finish_requester, 0)
@@ -222,12 +328,15 @@
     dk_sum[...] = dk[...]
     dv_sum[...] = dv[...]
 
-    def body(slot, _):
-        @pl.when(asked[slot] >= 0)
-        def _():
-            rows, cols = unit_place(asked[slot], blocks)
-            dk_sum[rows, cols] += returned[slot, :, :HD].astype(jnp.float32)
-            dv_sum[rows, cols] += returned[slot, :, HD:].astype(jnp.float32)
+    def body(target, _):
+        for slot in range(CAP):
+            unit = asked[target, 0, slot]
+
+            @pl.when(unit >= 0)
+            def _():
+                rows, cols = unit_place(unit, blocks)
+                dk_sum[rows, cols] += returned[target, slot, :, :HD].astype(jnp.float32)
+                dv_sum[rows, cols] += returned[target, slot, :, HD:].astype(jnp.float32)
 
         return 0
 
@@ -246,42 +355,49 @@
     heads, blocks, _ = selected.shape
     shards = lax.axis_size("seq")
     me = lax.axis_index("seq")
-    slots = shards * CAP
-    low = jax.ShapeDtypeStruct((slots, BLOCK, 2 * HD), jnp.bfloat16)
     unit, mask, local = request_tables(selected, me, shards)
-    asked = lax.all_to_all(unit, "seq", split_axis=0, concat_axis=0, tiled=True).reshape(-1)
-    outgoing = pl.pallas_call(
-        functools.partial(pack_kernel, blocks),
-        out_shape=low,
-        in_specs=[SMEM, VMEM, VMEM],
-        out_specs=VMEM,
-        compiler_params=LIMIT,
-        name="pack",
-    )(asked, keys, values)
     products = out_grad.astype(jnp.float32) * outputs.astype(jnp.float32)
     delta = jnp.sum(products.reshape(tokens, heads, HD), axis=-1).T
     wide = jax.ShapeDtypeStruct((tokens, width), jnp.float32)
     paired = (shards, CAP, BLOCK, 2 * HD)
-    dqt, dk, dv, returned = pl.pallas_call(
+    lanes_all = lax.axis_size("head")
+    stripe = tokens // lanes_all
+    width_in = w_query.shape[0]
+    piece = min(512, width_in)
+    pieces = width_in // piece
+    split = (pieces, lanes_all, stripe, piece)
+    x_grad, dk, dv, returned, asked = pl.pallas_call(
         exchange_kernel,
         out_shape=(
-            jax.ShapeDtypeStruct((heads, HD, tokens), jnp.bfloat16),
+            jax.ShapeDtypeStruct((stripe, width_in), jnp.bfloat16),
             wide,
             wide,
             jax.ShapeDtypeStruct(paired, jnp.bfloat16),
+            jax.ShapeDtypeStruct((shards, 1, HD), jnp.int32),
         ),
-        in_specs=[SMEM] * 3 + [VMEM] * 7,
-        out_specs=(VMEM,) * 4,
+        in_specs=[SMEM] * 3 + [VMEM] * 7 + [pl.BlockSpec(memory_space=pl.ANY)],
+        out_specs=(VMEM,) * 5,
         scratch_shapes=[
+            pltpu.VMEM(paired, jnp.bfloat16),
+            pltpu.VMEM((heads * blocks, BLOCK, 2 * HD), jnp.bfloat16),
+            pltpu.SMEM((shards, 1, HD), jnp.int32),
             pltpu.VMEM(paired, jnp.bfloat16),
             pltpu.VMEM(paired, jnp.bfloat16),
             pltpu.VMEM((heads, HD, tokens), jnp.float32),
             pltpu.VMEM((heads, tokens, HD), jnp.bfloat16),
             pltpu.VMEM((heads, tokens, HD), jnp.bfloat16),
+            pltpu.VMEM((width_in, width), jnp.bfloat16),
+            pltpu.VMEM((tokens, width), jnp.bfloat16),
+            pltpu.VMEM(split, jnp.bfloat16),
+            pltpu.VMEM(split, jnp.bfloat16),
+            pltpu.VMEM(split, jnp.float32),
         ]
-        + [pltpu.SemaphoreType.DMA((shards,))] * 4,
+        + [pltpu.SemaphoreType.DMA((shards,))] * 4
+        + [pltpu.SemaphoreType.DMA((pieces, lanes_all))] * 2
+        + [pltpu.SemaphoreType.DMA((shards,))] * 2
+        + [pltpu.SemaphoreType.DMA] * 2,
         compiler_params=pltpu.CompilerParams(
-            vmem_limit_bytes=48 * 2**20, collective_id=0, has_side_effects=True
+            vmem_limit_bytes=56 * 2**20, collective_id=0, has_side_effects=True
         ),
         name="exchange",
     )(
@@ -294,9 +410,9 @@
         out_grad,
         log_sum[:, None, :],
         delta[:, None, :],
-        outgoing.reshape(paired),
+        jnp.pad(unit[:, None, :], ((0, 0), (0, 0), (0, HD - CAP)), constant_values=-1),
+        w_query,
     )
-    returned = returned.reshape(slots, BLOCK, 2 * HD)
     result = jax.ShapeDtypeStruct((tokens, width), jnp.bfloat16)
     key_gradient, value_gradient = pl.pallas_call(
         functools.partial(settle_kernel, blocks),
@@ -307,12 +423,6 @@
         compiler_params=LIMIT,
         name="settle",
     )(asked, returned, dk, dv)
-    x_grad = lax.psum_scatter(
-        dot(dqt.reshape(width, tokens), w_query, (((0,), (1,)), ((), ()))),
-        "head",
-        scatter_dimension=0,
-        tiled=True,
-    ).astype(jnp.bfloat16)
     return x_grad, key_gradient, value_gradient
 
 

time: 288 us -> 180 us (0.62)
  waiting for transfers between devices: 64.9 us -> 0 us
  between operations: 14.2 us -> 0.76 us
  starting transfers between devices: 11.6 us -> 0 us
  Pallas kernels: 172 us -> 163 us
  matrix products: 4.37 us -> 0 us
  other arithmetic: 9.65 us -> 6.13 us
    reduce_scatter x1 -> x0, waiting for transfers between devices: 63 us -> none  [per_device(): lax.psum_scatter(dot(dqt.reshape(width, tokens), w_query, (((0,), (1,)),...]
    all_to_all x1 -> x0, starting transfers between devices: 11.6 us -> none  [per_device(): lax.all_to_all(unit, 'seq', split_axis=0, concat_axis=0, tiled=True)]
    pallas_call x2 -> x1, Pallas kernels: 165 us -> 156 us  [per_device(): pl.pallas_call(exchange_kernel, out_shape=(jax.ShapeDtypeStruct((stripe,...]
    dot_general x1 -> x0, matrix products: 4.37 us -> none  [dot(): return lax.dot_general(a, b, dims, preferred_element_type=jnp.float32)]
    unnamed x21 -> x8, local copies, waits for them, and re-layouts: 6.23 us -> 5.27 us
  transfers between devices with their start and end apart: 2 -> 0, of which waited for: 2 -> 0; matrix products, arithmetic and copies ran while one was open for 2% -> 0% of each run, Pallas kernels for 2% -> 0%
where the time goes in v2:
time: 180 us
  Pallas kernels  163 us (91%)
  local copies, waits for them, and re-layouts  9.98 us (6%)
  other arithmetic  6.13 us (3%)
    pallas_call x1, Pallas kernels, per_device(): pl.pallas_call(exchange_kernel, out_shape=(jax.ShapeDtypeStruct((stripe,...  156 us
    pallas_call x1, Pallas kernels, per_device(): pl.pallas_call(functools.partial(settle_kernel, blocks), out_shape=(resul...  6.56 us
    unnamed x8, local copies, waits for them, and re-layouts  5.27 us

profile of v2, /device:TPU:34, one launch (start us, length us, event | category | flops | bytes accessed | tf_op | source)
XLA Modules:
  0.0 179.7 jit_solution(9939485088671859950)
XLA Ops:
  0.7 1.3 broadcast_in_dim.133.logs
  2.0 0.9 fusion
  2.9 0.1 select_reduce_fusion.4
  3.0 0.1 copy.41
  3.1 0.1 copy.43
  3.2 1.4 select_reduce_fusion.2
  4.6 1.3 select_reduce_fusion.1
  6.0 0.1 copy.45
  6.1 0.6 reduce_sum.41.local
  6.7 0.1 copy.48
  6.8 0.1 copy.42
  6.9 0.1 concatenate.25
  7.0 0.6 and_select_fusion.picked
  7.6 0.1 copy.44
  7.7 0.7 reshape.144.mask
  8.3 0.1 copy.47
  8.5 0.1 broadcast_select_fusion
  8.5 0.6 pad.4.asking
  9.2 1.4 multiply_bitcast_fusion
  10.6 0.2 copy.50
  10.8 0.3 reduce_sum.42
  11.1 0.1 copy.46
  11.2 0.6 broadcast_in_dim.134.deltas
  11.8 156.3 %exchange.1 = (bf16[64,4096]{1,0:T(8,128)(2,1)}, f32[256,1024]{1,0:T(8,128)}, f32[256,1024]{1,0:T(8,128)}, bf16[64,2,64,256]{3,2,1,0:T(8,128)(2,1)}, s32[64,1,128]{2,1,0:T(1,128)}) custom-call(s32[128]{0:T(128)} %and_select_fusion.picked, s32[128]{0:T(128)} %reshape.144.mask, s32[32]{0:T(128)} %reduce_sum.41.local, bf16[256,1024]{1,0:T(8,128)(2,1)} %queries.1, ...), custom_call_target="tpu_custom_call" | custom-call | tf_op jit(solution)/shard_map/exchange/pallas_call | solution.py:369
  168.1 0.0 copy-start
  168.1 1.2 copy-done
  169.3 0.0 copy-start.1
  169.3 1.2 copy-done.1
  170.6 0.0 copy-start.2
  170.6 0.8 copy-done.2
  171.3 6.6 %settle.1 = (bf16[256,1024]{1,0:T(8,128)(2,1)}, bf16[256,1024]{1,0:T(8,128)(2,1)}) custom-call(s32[64,1,128]{2,1,0:T(1,128)S(1)} %copy-done.2, bf16[64,2,64,256]{3,2,1,0:T(8,128)(2,1)} %get-tuple-element.12.returned, f32[256,1024]{1,0:T(8,128)S(1)} %copy-done, f32[256,1024]{1,0:T(8,128)S(1)} %copy-done.1), custom_call_target="tpu_custom_call" | custom-call | tf_op jit(solution)/shard_map/settle/pallas_call | solution.py:417
  177.9 1.9 %copy.52 = bf16[64,4096]{1,0:T(8,128)(2,1)} copy(bf16[64,4096]{1,0:T(8,128)(2,1)} %get-tuple-element.23) | data formatting | bytes 1048576
  (8 shorter events, 0.1 us)
Async XLA Ops:
  168.1 1.2 copy-start
  169.3 1.2 copy-start.1
  170.6 0.8 copy-start.2

commit v3 on v2

--- a/solution.py
+++ b/solution.py
@@ -8,6 +8,7 @@
 from jax.sharding import PartitionSpec as P
 
 CAP = 2
+WINDOW = 12
 HD = 128
 BLOCK = 64
 FAR = 1e30
@@ -20,31 +21,45 @@
     return lax.dot_general(a, b, dims, preferred_element_type=jnp.float32)
 
 
-def request_tables(selected, me, shards):
+def smallest(values):
+    return jnp.min(functools.reduce(jnp.minimum, values), axis=0, keepdims=True)
+
+
+def total_of(values):
+    return jnp.sum(functools.reduce(jnp.add, values), axis=0, keepdims=True)
+
+
+def request_tables(selected, me):
     heads, blocks, picks = selected.shape
     units = heads * blocks
-    every = jnp.arange(shards * blocks, dtype=jnp.int32)
-    hit = jnp.any(selected[:, :, :, None] == every, axis=2)
-    weight = (1 << jnp.arange(blocks, dtype=jnp.int32))[None, :, None]
-    bits = jnp.sum(jnp.where(hit, weight, 0), axis=1)
-    bits = bits.reshape(heads, shards, blocks).transpose(1, 0, 2).reshape(shards, units)
-    owners = jnp.arange(shards, dtype=jnp.int32)[:, None]
-    local = jnp.sum(jnp.where(owners == me, bits, 0), axis=0)
-    bits = jnp.where(owners == me, 0, bits)
-    index = jnp.arange(units, dtype=jnp.int32)
-    first = jnp.min(jnp.where(bits > 0, index, units), axis=1, keepdims=True)
-    second = jnp.min(jnp.where((bits > 0) & (index > first), index, units), axis=1, keepdims=True)
-    unit = jnp.concatenate((first, second), axis=1)
-    mask = jnp.sum(jnp.where(unit[:, :, None] == index, bits[:, None, :], 0), axis=2)
-    return jnp.where(unit == units, -1, unit), mask, local
-
-
-def unit_place(unit, blocks):
-    head = unit // blocks
-    return (
-        pl.ds(pl.multiple_of((unit - head * blocks) * BLOCK, BLOCK), BLOCK),
-        pl.ds(pl.multiple_of(head * HD, HD), HD),
-    )
+    lanes = lax.broadcasted_iota(jnp.int32, (heads, HD), 1)
+    head = lax.broadcasted_iota(jnp.int32, (heads, HD), 0)
+    bits = [jnp.zeros((heads, HD), jnp.int32) for _ in range(blocks)]
+    for query_block in range(blocks):
+        rows = selected[:, query_block, :]
+        hit = [jnp.zeros((heads, HD), jnp.bool_) for _ in range(blocks)]
+        for pick in range(picks):
+            entry = jnp.broadcast_to(rows[:, pick : pick + 1], (heads, HD))
+            for block in range(blocks):
+                hit[block] = hit[block] | (entry == lanes * blocks + block)
+        bits = [b + jnp.where(h, 1 << query_block, 0) for b, h in zip(bits, hit)]
+    own = jnp.zeros((heads, HD), jnp.int32)
+    for block in range(blocks):
+        mine = jnp.sum(jnp.where(lanes == me, bits[block], 0), axis=1, keepdims=True)
+        own = jnp.where(lanes == block, mine, own)
+    bits = [jnp.where(lanes == me, 0, b) for b in bits]
+    index = [head * blocks + block for block in range(blocks)]
+    first = smallest([jnp.where(b > 0, i, units) for b, i in zip(bits, index)])
+    second = smallest([jnp.where((b > 0) & (i > first), i, units) for b, i in zip(bits, index)])
+    rows = []
+    for at in (first, second):
+        rows.append(jnp.where(at == units, -1, at))
+    for at in (first, second):
+        rows.append(total_of([jnp.where(i == at, b, 0) for b, i in zip(bits, index)]))
+    for at in (first, second):
+        rows.append(total_of([jnp.where(i == at, head, 0) for i in index]))
+    rows += [jnp.zeros_like(first)] * 2
+    return jnp.concatenate(rows, axis=0), own
 
 
 def backward(key, value, query, grad, log_row, delta_row, allowed=None):
@@ -61,25 +76,28 @@
 
 
 def exchange_kernel(
-    picked,
-    mask,
-    local,
+    selected,
     queries,
     keys,
     values,
+    outputs,
     grads,
-    logs,
-    deltas,
-    asking,
+    log_sum,
     weight,
     x_grad,
     dk,
     dv,
+    logs,
+    deltas,
+    sums_here,
     returned,
     asked,
     outgoing,
     units_here,
     asked_here,
+    asking,
+    table,
+    table_here,
     pulled,
     back,
     total,
@@ -100,17 +118,26 @@
     ask_recv,
     weight_sem,
     asked_sem,
+    table_sem,
 ):
     me = lax.axis_index("seq")
     lane = lax.axis_index("head")
+    shards = asking.shape[0]
     lanes_all = parts_out.shape[1]
     stripe, piece = parts_out.shape[2:]
     pieces = parts_out.shape[0]
     weight_copy = pltpu.make_async_copy(weight, weight_here, weight_sem)
     weight_copy.start()
     asked[...] = jnp.full(asked.shape, -1, jnp.int32)
-    shards = asking.shape[0]
-    heads = logs.shape[0]
+    requests, own = request_tables(selected, me)
+    table[:8] = requests
+    table[8:] = own
+    table_copy = pltpu.make_async_copy(table, table_here, table_sem)
+    table_copy.start()
+    turned = jnp.concatenate([requests] + [jnp.zeros((HD - 8, HD), jnp.int32)], axis=0).T
+    for source in range(shards):
+        asking[source] = turned[source : source + 1, :]
+    heads = log_sum.shape[0]
     tokens = queries.shape[0]
     blocks = tokens // BLOCK
     lane_block = lax.broadcasted_iota(jnp.int32, (1, tokens), 1) // BLOCK
@@ -198,6 +225,7 @@
     asked_copy = pltpu.make_async_copy(asked, asked_here, asked_sem)
     asked_copy.start()
     asked_copy.wait()
+    table_copy.wait()
 
     def send(target):
         for slot in range(CAP):
@@ -217,7 +245,12 @@
 
         return 0
 
-    lax.fori_loop(1, shards, send_step, 0)
+    lax.fori_loop(1, min(WINDOW + 1, shards), send_step, 0)
+    for head in range(heads):
+        cols = slice(head * HD, (head + 1) * HD)
+        products = grads[:, cols].astype(jnp.float32) * outputs[:, cols].astype(jnp.float32)
+        deltas[head] = jnp.sum(products.T, axis=0, keepdims=True)
+        logs[head] = log_sum[head : head + 1, :]
 
     def open_logs(head, bits):
         return jnp.where(((bits >> lane_block) & 1) == 1, logs[head], FAR)
@@ -235,13 +268,13 @@
                 values[place, cols],
                 query,
                 grad,
-                open_logs(head, local[head * blocks + block]),
+                open_logs(head, table_here[8 + head, block]),
                 deltas[head],
                 rows + block * BLOCK <= lanes,
             )
             sums += dq
-            dk[place, cols] = dk_part
-            dv[place, cols] = dv_part
+            sums_here[head * blocks + block, :, :HD] = dk_part
+            sums_here[head * blocks + block, :, HD:] = dv_part
         total[head] = sums
         return 0
 
@@ -252,13 +285,13 @@
         pull_copy(source, source, source, source).wait_recv()
         parts = []
         for slot in range(CAP):
-            head = picked[source * CAP + slot]
+            head = table_here[2 * CAP + slot, source]
             dq, dk_part, dv_part = backward(
                 pulled[source, slot, :, :HD],
                 pulled[source, slot, :, HD:],
                 query_heads[head],
                 grad_heads[head],
-                open_logs(head, mask[source * CAP + slot]),
+                open_logs(head, table_here[CAP + slot, source]),
                 deltas[head],
             )
             back[source, slot, :, :HD] = dk_part.astype(jnp.bfloat16)
@@ -274,6 +307,15 @@
     def source_step(step, _):
         offset = offset_of(step, shards)
 
+        @pl.when(me + offset < shards)
+        def _():
+            sent = me + offset
+            pull_copy(sent, sent, sent, sent).wait_send()
+
+        @pl.when(step + WINDOW < shards)
+        def _():
+            send_step(step + WINDOW, 0)
+
         @pl.when(offset <= me)
         def _():
             one_source(offset, 0)
@@ -297,6 +339,34 @@
 
     lax.fori_loop(0, pieces, one_piece, 0)
 
+    def one_return(step, _):
+        target = me + offset_of(step, shards)
+
+        @pl.when(target < shards)
+        def _():
+            back_copy(target, target, target, target).wait_recv()
+            first, second = (jnp.full((BLOCK, 2 * HD), asked_here[target, 0, i]) for i in range(CAP))
+
+            def one_unit(unit, _):
+                late = jnp.where(second == unit, returned[target, 1].astype(jnp.float32), 0.0)
+                sums_here[unit] += jnp.where(
+                    first == unit, returned[target, 0].astype(jnp.float32), late
+                )
+                return 0
+
+            lax.fori_loop(0, heads * blocks, one_unit, 0, unroll=4)
+
+        return 0
+
+    lax.fori_loop(1, shards, one_return, 0)
+    for head in range(heads):
+        cols = slice(head * HD, (head + 1) * HD)
+        for block in range(blocks):
+            rows = slice(block * BLOCK, (block + 1) * BLOCK)
+            both = sums_here[head * blocks + block].astype(jnp.bfloat16)
+            dk[rows, cols] = both[:, :HD]
+            dv[rows, cols] = both[:, HD:]
+
     def one_sum(at, _):
         row_sum = own_part[at, lane]
         for step in range(1, lanes_all):
@@ -309,13 +379,6 @@
 
     lax.fori_loop(0, pieces, one_sum, 0)
 
-    def finish_owner(target, _):
-        pull_copy(target, target, target, target).wait_send()
-        back_copy(target, target, target, target).wait_recv()
-        return 0
-
-    lax.fori_loop(me + 1, shards, finish_owner, 0)
-
     def finish_requester(source, _):
         back_copy(source, source, source, source).wait_send()
         ask_copy(source, source, source, source).wait_send()
@@ -324,41 +387,14 @@
     lax.fori_loop(0, me, finish_requester, 0)
 
 
-def settle_kernel(blocks, asked, returned, dk, dv, dk_out, dv_out, dk_sum, dv_sum):
-    dk_sum[...] = dk[...]
-    dv_sum[...] = dv[...]
-
-    def body(target, _):
-        for slot in range(CAP):
-            unit = asked[target, 0, slot]
-
-            @pl.when(unit >= 0)
-            def _():
-                rows, cols = unit_place(unit, blocks)
-                dk_sum[rows, cols] += returned[target, slot, :, :HD].astype(jnp.float32)
-                dv_sum[rows, cols] += returned[target, slot, :, HD:].astype(jnp.float32)
-
-        return 0
-
-    lax.fori_loop(0, returned.shape[0], body, 0)
-    dk_out[...] = dk_sum[...].astype(jnp.bfloat16)
-    dv_out[...] = dv_sum[...].astype(jnp.bfloat16)
-
-
-SMEM = pl.BlockSpec(memory_space=pltpu.SMEM)
 VMEM = pl.BlockSpec(memory_space=pltpu.VMEM)
-LIMIT = pltpu.CompilerParams(vmem_limit_bytes=48 * 2**20)
 
 
 def per_device(queries, keys, values, outputs, out_grad, log_sum, selected, w_query):
     tokens, width = queries.shape
     heads, blocks, _ = selected.shape
     shards = lax.axis_size("seq")
-    me = lax.axis_index("seq")
-    unit, mask, local = request_tables(selected, me, shards)
-    products = out_grad.astype(jnp.float32) * outputs.astype(jnp.float32)
-    delta = jnp.sum(products.reshape(tokens, heads, HD), axis=-1).T
-    wide = jax.ShapeDtypeStruct((tokens, width), jnp.float32)
+    result = jax.ShapeDtypeStruct((tokens, width), jnp.bfloat16)
     paired = (shards, CAP, BLOCK, 2 * HD)
     lanes_all = lax.axis_size("head")
     stripe = tokens // lanes_all
@@ -366,21 +402,27 @@
     piece = min(512, width_in)
     pieces = width_in // piece
     split = (pieces, lanes_all, stripe, piece)
-    x_grad, dk, dv, returned, asked = pl.pallas_call(
+    return pl.pallas_call(
         exchange_kernel,
         out_shape=(
             jax.ShapeDtypeStruct((stripe, width_in), jnp.bfloat16),
-            wide,
-            wide,
-            jax.ShapeDtypeStruct(paired, jnp.bfloat16),
-            jax.ShapeDtypeStruct((shards, 1, HD), jnp.int32),
+            result,
+            result,
         ),
-        in_specs=[SMEM] * 3 + [VMEM] * 7 + [pl.BlockSpec(memory_space=pl.ANY)],
-        out_specs=(VMEM,) * 5,
+        in_specs=[VMEM] * 7 + [pl.BlockSpec(memory_space=pl.ANY)],
+        out_specs=(VMEM,) * 3,
         scratch_shapes=[
+            pltpu.VMEM((heads, 1, tokens), jnp.float32),
+            pltpu.VMEM((heads, 1, tokens), jnp.float32),
+            pltpu.VMEM((heads * blocks, BLOCK, 2 * HD), jnp.float32),
+            pltpu.VMEM(paired, jnp.bfloat16),
+            pltpu.VMEM((shards, 1, HD), jnp.int32),
             pltpu.VMEM(paired, jnp.bfloat16),
             pltpu.VMEM((heads * blocks, BLOCK, 2 * HD), jnp.bfloat16),
             pltpu.SMEM((shards, 1, HD), jnp.int32),
+            pltpu.VMEM((shards, 1, HD), jnp.int32),
+            pltpu.VMEM((8 + heads, HD), jnp.int32),
+            pltpu.SMEM((8 + heads, HD), jnp.int32),
             pltpu.VMEM(paired, jnp.bfloat16),
             pltpu.VMEM(paired, jnp.bfloat16),
             pltpu.VMEM((heads, HD, tokens), jnp.float32),
@@ -395,35 +437,21 @@
         + [pltpu.SemaphoreType.DMA((shards,))] * 4
         + [pltpu.SemaphoreType.DMA((pieces, lanes_all))] * 2
         + [pltpu.SemaphoreType.DMA((shards,))] * 2
-        + [pltpu.SemaphoreType.DMA] * 2,
+        + [pltpu.SemaphoreType.DMA] * 3,
         compiler_params=pltpu.CompilerParams(
             vmem_limit_bytes=56 * 2**20, collective_id=0, has_side_effects=True
         ),
         name="exchange",
     )(
-        jnp.maximum(unit.reshape(-1), 0) // blocks,
-        mask.reshape(-1),
-        local,
+        selected,
         queries,
         keys,
         values,
+        outputs,
         out_grad,
-        log_sum[:, None, :],
-        delta[:, None, :],
-        jnp.pad(unit[:, None, :], ((0, 0), (0, 0), (0, HD - CAP)), constant_values=-1),
+        log_sum,
         w_query,
     )
-    result = jax.ShapeDtypeStruct((tokens, width), jnp.bfloat16)
-    key_gradient, value_gradient = pl.pallas_call(
-        functools.partial(settle_kernel, blocks),
-        out_shape=(result, result),
-        in_specs=[SMEM] + [VMEM] * 3,
-        out_specs=(VMEM, VMEM),
-        scratch_shapes=[pltpu.VMEM((tokens, width), jnp.float32)] * 2,
-        compiler_params=LIMIT,
-        name="settle",
-    )(asked, returned, dk, dv)
-    return x_grad, key_gradient, value_gradient
 
 
 def solution(mesh):

time: 180 us -> 153 us (0.85)
  the two profiles are of different devices: /device:TPU:34 before, /device:TPU:225 now
where the time goes in v3:
time: 153 us
  Pallas kernels  147 us (96%)
  local copies, waits for them, and re-layouts  5.6 us (4%)
    pallas_call x1, Pallas kernels, per_device(): pl.pallas_call(exchange_kernel, out_shape=(jax.ShapeDtypeStruct((stripe,...  147 us
    unnamed x3, local copies, waits for them, and re-layouts  5.6 us

profile of v3, /device:TPU:225, one launch (start us, length us, event | category | flops | bytes accessed | tf_op | source)
XLA Modules:
  0.0 152.8 jit_solution(9647051806589995892)
XLA Ops:
  0.6 146.6 %exchange.1 = (bf16[64,4096]{1,0:T(8,128)(2,1)}, bf16[256,1024]{1,0:T(8,128)(2,1)}, bf16[256,1024]{1,0:T(8,128)(2,1)}) custom-call(s32[8,4,16]{2,1,0:T(4,128)} %selected.1, bf16[256,1024]{1,0:T(8,128)(2,1)} %queries.1, bf16[256,1024]{1,0:T(8,128)(2,1)} %keys.1, bf16[256,1024]{1,0:T(8,128)(2,1)} %values.1, bf16[256,1024]{1,0:T(8,128)(2,1)} %outputs.1, ...), custom_call_target="tpu_custom_call" | custom-call | tf_op jit(solution)/shard_map/exchange/pallas_call | solution.py:405
  147.2 1.9 %copy.14 = bf16[64,4096]{1,0:T(8,128)(2,1)} copy(bf16[64,4096]{1,0:T(8,128)(2,1)} %get-tuple-element.6) | data formatting | bytes 1048576
  149.1 1.9 %copy.15 = bf16[256,1024]{1,0:T(8,128)(2,1)} copy(bf16[256,1024]{1,0:T(8,128)(2,1)} %get-tuple-element.7) | data formatting | bytes 1048576
  151.0 1.9 %copy.16 = bf16[256,1024]{1,0:T(8,128)(2,1)} copy(bf16[256,1024]{1,0:T(8,128)(2,1)} %get-tuple-element.8) | data formatting | bytes 1048576

commit v4 on v3

--- a/solution.py
+++ b/solution.py
@@ -9,6 +9,7 @@
 
 CAP = 2
 WINDOW = 12
+LAG = 16
 HD = 128
 BLOCK = 64
 FAR = 1e30
@@ -107,6 +108,7 @@
     dq_rows,
     parts_out,
     parts_in,
+    relay_in,
     own_part,
     pull_send,
     pull_recv,
@@ -114,6 +116,7 @@
     back_recv,
     part_send,
     part_recv,
+    relay_recv,
     ask_send,
     ask_recv,
     weight_sem,
@@ -124,11 +127,86 @@
     lane = lax.axis_index("head")
     shards = asking.shape[0]
     lanes_all = parts_out.shape[1]
+    up, far, down = (lax.rem(lane + step, lanes_all) for step in (1, 2, 3))
     stripe, piece = parts_out.shape[2:]
     pieces = parts_out.shape[0]
+    asked[...] = jnp.full(asked.shape, -1, jnp.int32)
+    heads = log_sum.shape[0]
+    tokens = queries.shape[0]
+    blocks = tokens // BLOCK
+    lane_block = lax.broadcasted_iota(jnp.int32, (1, tokens), 1) // BLOCK
+
+    def pull_copy(slot_from, slot_to, target, index):
+        return pltpu.make_async_remote_copy(
+            src_ref=outgoing.at[slot_from],
+            dst_ref=pulled.at[slot_to],
+            send_sem=pull_send.at[slot_from],
+            recv_sem=pull_recv.at[index],
+            device_id={"seq": target},
+            device_id_type=pl.DeviceIdType.MESH,
+        )
+
+    def back_copy(slot_from, slot_to, target, index):
+        return pltpu.make_async_remote_copy(
+            src_ref=back.at[slot_from],
+            dst_ref=returned.at[slot_to],
+            send_sem=back_send.at[slot_from],
+            recv_sem=back_recv.at[index],
+            device_id={"seq": target},
+            device_id_type=pl.DeviceIdType.MESH,
+        )
+
+    def ask_copy(slot_from, slot_to, target, index):
+        return pltpu.make_async_remote_copy(
+            src_ref=asking.at[slot_from],
+            dst_ref=asked.at[slot_to],
+            send_sem=ask_send.at[slot_from],
+            recv_sem=ask_recv.at[index],
+            device_id={"seq": target},
+            device_id_type=pl.DeviceIdType.MESH,
+        )
+
+    def relay_copy(at, slot, target):
+        return pltpu.make_async_remote_copy(
+            src_ref=parts_out.at[at, slot],
+            dst_ref=relay_in.at[at],
+            send_sem=part_send.at[at, slot],
+            recv_sem=relay_recv.at[at],
+            device_id={"head": target},
+            device_id_type=pl.DeviceIdType.MESH,
+        )
+
+    def part_copy(at, target, side):
+        return pltpu.make_async_remote_copy(
+            src_ref=parts_out.at[at, target],
+            dst_ref=parts_in.at[at, side],
+            send_sem=part_send.at[at, target],
+            recv_sem=part_recv.at[at, side],
+            device_id={"head": target},
+            device_id_type=pl.DeviceIdType.MESH,
+        )
+
+    barrier = pltpu.get_barrier_semaphore()
+
+    def greet(step, _):
+        pl.semaphore_signal(
+            barrier,
+            inc=1,
+            device_id={"seq": lax.rem(me + step, shards)},
+            device_id_type=pl.DeviceIdType.MESH,
+        )
+        return 0
+
+    lax.fori_loop(1, shards, greet, 0)
+    for neighbour in (up, down):
+        pl.semaphore_signal(
+            barrier,
+            inc=1,
+            device_id={"head": neighbour},
+            device_id_type=pl.DeviceIdType.MESH,
+        )
     weight_copy = pltpu.make_async_copy(weight, weight_here, weight_sem)
     weight_copy.start()
-    asked[...] = jnp.full(asked.shape, -1, jnp.int32)
     requests, own = request_tables(selected, me)
     table[:8] = requests
     table[8:] = own
@@ -137,71 +215,7 @@
     turned = jnp.concatenate([requests] + [jnp.zeros((HD - 8, HD), jnp.int32)], axis=0).T
     for source in range(shards):
         asking[source] = turned[source : source + 1, :]
-    heads = log_sum.shape[0]
-    tokens = queries.shape[0]
-    blocks = tokens // BLOCK
-    lane_block = lax.broadcasted_iota(jnp.int32, (1, tokens), 1) // BLOCK
-
-    def pull_copy(slot_from, slot_to, target, index):
-        return pltpu.make_async_remote_copy(
-            src_ref=outgoing.at[slot_from],
-            dst_ref=pulled.at[slot_to],
-            send_sem=pull_send.at[slot_from],
-            recv_sem=pull_recv.at[index],
-            device_id={"seq": target},
-            device_id_type=pl.DeviceIdType.MESH,
-        )
-
-    def back_copy(slot_from, slot_to, target, index):
-        return pltpu.make_async_remote_copy(
-            src_ref=back.at[slot_from],
-            dst_ref=returned.at[slot_to],
-            send_sem=back_send.at[slot_from],
-            recv_sem=back_recv.at[index],
-            device_id={"seq": target},
-            device_id_type=pl.DeviceIdType.MESH,
-        )
-
-    def ask_copy(slot_from, slot_to, target, index):
-        return pltpu.make_async_remote_copy(
-            src_ref=asking.at[slot_from],
-            dst_ref=asked.at[slot_to],
-            send_sem=ask_send.at[slot_from],
-            recv_sem=ask_recv.at[index],
-            device_id={"seq": target},
-            device_id_type=pl.DeviceIdType.MESH,
-        )
-
-    def part_copy(at, slot_from, slot_to, target, index):
-        return pltpu.make_async_remote_copy(
-            src_ref=parts_out.at[at, slot_from],
-            dst_ref=parts_in.at[at, slot_to],
-            send_sem=part_send.at[at, slot_from],
-            recv_sem=part_recv.at[at, index],
-            device_id={"head": target},
-            device_id_type=pl.DeviceIdType.MESH,
-        )
-
-    barrier = pltpu.get_barrier_semaphore()
-
-    def greet(step, _):
-        pl.semaphore_signal(
-            barrier,
-            inc=1,
-            device_id={"seq": lax.rem(me + step, shards)},
-            device_id_type=pl.DeviceIdType.MESH,
-        )
-        return 0
-
-    lax.fori_loop(1, shards, greet, 0)
-    for step in range(1, lanes_all):
-        pl.semaphore_signal(
-            barrier,
-            inc=1,
-            device_id={"head": lax.rem(lane + step, lanes_all)},
-            device_id_type=pl.DeviceIdType.MESH,
-        )
-    pl.semaphore_wait(barrier, shards - 1 + lanes_all - 1)
+    pl.semaphore_wait(barrier, shards - 1 + 2)
 
     def ask(source, _):
         ask_copy(source, me, source, me).start()
@@ -304,41 +318,6 @@
             )
         return 0
 
-    def source_step(step, _):
-        offset = offset_of(step, shards)
-
-        @pl.when(me + offset < shards)
-        def _():
-            sent = me + offset
-            pull_copy(sent, sent, sent, sent).wait_send()
-
-        @pl.when(step + WINDOW < shards)
-        def _():
-            send_step(step + WINDOW, 0)
-
-        @pl.when(offset <= me)
-        def _():
-            one_source(offset, 0)
-
-        return 0
-
-    lax.fori_loop(1, shards, source_step, 0)
-    for head in range(heads):
-        dq_rows[:, head * HD : (head + 1) * HD] = (total[head] * HD**-0.5).T.astype(jnp.bfloat16)
-    weight_copy.wait()
-
-    def one_piece(at, _):
-        columns = pl.ds(pl.multiple_of(at * piece, piece), piece)
-        product = dot(dq_rows[...], weight_here[columns, :], NT).reshape(lanes_all, stripe, piece)
-        own_part[at] = product
-        parts_out[at] = product.astype(jnp.bfloat16)
-        for step in range(1, lanes_all):
-            target = lax.rem(lane + step, lanes_all)
-            part_copy(at, target, lane, target, lane).start()
-        return 0
-
-    lax.fori_loop(0, pieces, one_piece, 0)
-
     def one_return(step, _):
         target = me + offset_of(step, shards)
 
@@ -358,7 +337,70 @@
 
         return 0
 
-    lax.fori_loop(1, shards, one_return, 0)
+    def source_step(step, _):
+        offset = offset_of(step, shards)
+
+        @pl.when(me + offset < shards)
+        def _():
+            sent = me + offset
+            pull_copy(sent, sent, sent, sent).wait_send()
+
+        @pl.when(step + WINDOW < shards)
+        def _():
+            send_step(step + WINDOW, 0)
+
+        @pl.when(offset <= me)
+        def _():
+            one_source(offset, 0)
+
+        @pl.when(step > LAG)
+        def _():
+            one_return(step - LAG, 0)
+
+        return 0
+
+    lax.fori_loop(1, shards, source_step, 0)
+    for head in range(heads):
+        dq_rows[:, head * HD : (head + 1) * HD] = (total[head] * HD**-0.5).T.astype(jnp.bfloat16)
+    weight_copy.wait()
+
+    half = pieces // 2
+
+    def one_piece(at, toward):
+        columns = pl.ds(pl.multiple_of(at * piece, piece), piece)
+        product = dot(dq_rows[...], weight_here[columns, :], NT).reshape(lanes_all, stripe, piece)
+        own_part[at] = product
+        parts_out[at] = product.astype(jnp.bfloat16)
+        relay_copy(at, far, toward).start()
+
+    def two_pieces(at, _):
+        one_piece(at, up)
+        one_piece(half + at, down)
+        return 0
+
+    lax.fori_loop(0, half, two_pieces, 0)
+
+    def two_direct(at, _):
+        part_copy(at, down, 1).start()
+        part_copy(half + at, up, 0).start()
+        return 0
+
+    lax.fori_loop(0, half, two_direct, 0)
+
+    def one_relay(at, target, origin, side):
+        relay_copy(at, far, origin).wait_recv()
+        joined = own_part[at, target] + relay_in[at].astype(jnp.float32)
+        parts_out[at, target] = joined.astype(jnp.bfloat16)
+        part_copy(at, target, side).start()
+
+    def two_relays(at, _):
+        one_relay(at, up, down, 0)
+        one_relay(half + at, down, up, 1)
+        return 0
+
+    lax.fori_loop(0, half, two_relays, 0)
+
+    lax.fori_loop(max(1, shards - LAG), shards, one_return, 0)
     for head in range(heads):
         cols = slice(head * HD, (head + 1) * HD)
         for block in range(blocks):
@@ -369,10 +411,10 @@
 
     def one_sum(at, _):
         row_sum = own_part[at, lane]
-        for step in range(1, lanes_all):
-            source = lax.rem(lane + step, lanes_all)
-            part_copy(at, source, source, source, source).wait()
-            row_sum += parts_in[at, source].astype(jnp.float32)
+        for side, target in ((0, up), (1, down)):
+            part_copy(at, target, side).wait()
+            row_sum += parts_in[at, side].astype(jnp.float32)
+        relay_copy(at, far, up).wait_send()
         columns = pl.ds(pl.multiple_of(at * piece, piece), piece)
         x_grad[:, columns] = row_sum.astype(jnp.bfloat16)
         return 0
@@ -385,6 +427,11 @@
         return 0
 
     lax.fori_loop(0, me, finish_requester, 0)
+
+
+def hand_out_kernel(*refs):
+    for given, result in zip(refs[:3], refs[3:]):
+        result[...] = given[...]
 
 
 VMEM = pl.BlockSpec(memory_space=pltpu.VMEM)
@@ -399,10 +446,10 @@
     lanes_all = lax.axis_size("head")
     stripe = tokens // lanes_all
     width_in = w_query.shape[0]
-    piece = min(512, width_in)
+    piece = min(512, width_in // 2)
     pieces = width_in // piece
     split = (pieces, lanes_all, stripe, piece)
-    return pl.pallas_call(
+    arrays = pl.pallas_call(
         exchange_kernel,
         out_shape=(
             jax.ShapeDtypeStruct((stripe, width_in), jnp.bfloat16),
@@ -431,11 +478,13 @@
             pltpu.VMEM((width_in, width), jnp.bfloat16),
             pltpu.VMEM((tokens, width), jnp.bfloat16),
             pltpu.VMEM(split, jnp.bfloat16),
-            pltpu.VMEM(split, jnp.bfloat16),
+            pltpu.VMEM((pieces, 2, stripe, piece), jnp.bfloat16),
+            pltpu.VMEM((pieces, stripe, piece), jnp.bfloat16),
             pltpu.VMEM(split, jnp.float32),
         ]
         + [pltpu.SemaphoreType.DMA((shards,))] * 4
-        + [pltpu.SemaphoreType.DMA((pieces, lanes_all))] * 2
+        + [pltpu.SemaphoreType.DMA((pieces, lanes_all)), pltpu.SemaphoreType.DMA((pieces, 2))]
+        + [pltpu.SemaphoreType.DMA((pieces,))]
         + [pltpu.SemaphoreType.DMA((shards,))] * 2
         + [pltpu.SemaphoreType.DMA] * 3,
         compiler_params=pltpu.CompilerParams(
@@ -452,6 +501,13 @@
         log_sum,
         w_query,
     )
+    return pl.pallas_call(
+        hand_out_kernel,
+        out_shape=tuple(jax.ShapeDtypeStruct(a.shape, a.dtype) for a in arrays),
+        in_specs=[VMEM] * 3,
+        out_specs=(VMEM,) * 3,
+        name="hand_out",
+    )(*arrays)
 
 
 def solution(mesh):

time: 153 us -> 144 us (0.941)
  the two profiles are of different devices: /device:TPU:225 before, /device:TPU:4 now
where the time goes in v4:
time: 144 us
  Pallas kernels  144 us (100%)
    pallas_call x1, Pallas kernels, per_device(): pl.pallas_call(exchange_kernel, out_shape=(jax.ShapeDtypeStruct((stripe,...  141 us

profile of v4, /device:TPU:4, one launch (start us, length us, event | category | flops | bytes accessed | tf_op | source)
XLA Modules:
  0.0 144.3 jit_solution(8105241259889978912)
XLA Ops:
  0.6 141.1 %exchange.1 = (bf16[64,4096]{1,0:T(8,128)(2,1)}, bf16[256,1024]{1,0:T(8,128)(2,1)}, bf16[256,1024]{1,0:T(8,128)(2,1)}) custom-call(s32[8,4,16]{2,1,0:T(4,128)} %selected.1, bf16[256,1024]{1,0:T(8,128)(2,1)} %queries.1, bf16[256,1024]{1,0:T(8,128)(2,1)} %keys.1, bf16[256,1024]{1,0:T(8,128)(2,1)} %values.1, bf16[256,1024]{1,0:T(8,128)(2,1)} %outputs.1, ...), custom_call_target="tpu_custom_call" | custom-call | tf_op jit(solution)/shard_map/exchange/pallas_call | solution.py:452
  141.8 2.5 %hand_out.1 = (bf16[64,4096]{1,0:T(8,128)(2,1)}, bf16[256,1024]{1,0:T(8,128)(2,1)}, bf16[256,1024]{1,0:T(8,128)(2,1)}) custom-call(bf16[64,4096]{1,0:T(8,128)(2,1)} %get-tuple-element.6.refs_0_, bf16[256,1024]{1,0:T(8,128)(2,1)} %get-tuple-element.7.refs_1_, bf16[256,1024]{1,0:T(8,128)(2,1)} %get-tuple-element.8.refs_2_), custom_call_target="tpu_custom_call" | custom-call | tf_op jit(solution)/shard_map/hand_out/pallas_call | solution.py:504

commit v5 on v4

--- a/solution.py
+++ b/solution.py
@@ -8,8 +8,8 @@
 from jax.sharding import PartitionSpec as P
 
 CAP = 2
-WINDOW = 12
-LAG = 16
+WINDOW = 14
+LAG = 20
 HD = 128
 BLOCK = 64
 FAR = 1e30
@@ -78,24 +78,31 @@
 
 def exchange_kernel(
     selected,
+    queries_far,
+    keys_far,
+    values_far,
+    outputs_far,
+    grads_far,
+    log_sum,
+    weight,
+    x_grad,
+    dk,
+    dv,
     queries,
     keys,
     values,
     outputs,
     grads,
-    log_sum,
-    weight,
-    x_grad,
-    dk,
-    dv,
     logs,
     deltas,
     sums_here,
     returned,
     asked,
+    asked_late,
     outgoing,
     units_here,
     asked_here,
+    asked_late_here,
     asking,
     table,
     table_here,
@@ -122,6 +129,8 @@
     weight_sem,
     asked_sem,
     table_sem,
+    load_sem,
+    late_sem,
 ):
     me = lax.axis_index("seq")
     lane = lax.axis_index("head")
@@ -131,6 +140,12 @@
     stripe, piece = parts_out.shape[2:]
     pieces = parts_out.shape[0]
     asked[...] = jnp.full(asked.shape, -1, jnp.int32)
+    asked_late[...] = jnp.full(asked.shape, -1, jnp.int32)
+    far_refs = (keys_far, values_far, queries_far, grads_far, outputs_far)
+    near_refs = (keys, values, queries, grads, outputs)
+    loads = [
+        pltpu.make_async_copy(*pair, load_sem.at[i]) for i, pair in enumerate(zip(far_refs, near_refs))
+    ]
     heads = log_sum.shape[0]
     tokens = queries.shape[0]
     blocks = tokens // BLOCK
@@ -156,10 +171,12 @@
             device_id_type=pl.DeviceIdType.MESH,
         )
 
-    def ask_copy(slot_from, slot_to, target, index):
+    early = min(WINDOW + 1, shards)
+
+    def ask_copy(landing, slot_from, slot_to, target, index):
         return pltpu.make_async_remote_copy(
             src_ref=asking.at[slot_from],
-            dst_ref=asked.at[slot_to],
+            dst_ref=landing.at[slot_to],
             send_sem=ask_send.at[slot_from],
             recv_sem=ask_recv.at[index],
             device_id={"seq": target},
@@ -205,6 +222,8 @@
             device_id={"head": neighbour},
             device_id_type=pl.DeviceIdType.MESH,
         )
+    for load in loads:
+        load.start()
     weight_copy = pltpu.make_async_copy(weight, weight_here, weight_sem)
     weight_copy.start()
     requests, own = request_tables(selected, me)
@@ -217,49 +236,65 @@
         asking[source] = turned[source : source + 1, :]
     pl.semaphore_wait(barrier, shards - 1 + 2)
 
-    def ask(source, _):
-        ask_copy(source, me, source, me).start()
-        return 0
-
-    lax.fori_loop(0, me, ask, 0)
+    def ask(landing, step, _):
+        source = me - offset_of(step, shards)
+
+        @pl.when(source >= 0)
+        def _():
+            ask_copy(landing, source, me, source, me).start()
+
+        return 0
+
+    def heard(landing, step, _):
+        target = me + offset_of(step, shards)
+
+        @pl.when(target < shards)
+        def _():
+            ask_copy(landing, target, target, target, target).wait_recv()
+
+        return 0
+
+    def send_step(wanted_here, step, _):
+        target = me + offset_of(step, shards)
+
+        @pl.when(target < shards)
+        def _():
+            for slot in range(CAP):
+                wanted = wanted_here[target, 0, slot]
+                found = units_here[jnp.maximum(wanted, 0)]
+                outgoing[target, slot] = jnp.where(
+                    jnp.full(found.shape, wanted, jnp.int32) >= 0, found, jnp.zeros_like(found)
+                )
+            pull_copy(target, me, target, me).start()
+
+        return 0
+
+    lax.fori_loop(1, early, functools.partial(ask, asked), 0)
+    for load in loads[:2]:
+        load.wait()
+    for head in range(heads):
+        cols = slice(head * HD, (head + 1) * HD)
+        for block in range(blocks):
+            rows = slice(block * BLOCK, (block + 1) * BLOCK)
+            units_here[head * blocks + block, :, :HD] = keys[rows, cols]
+            units_here[head * blocks + block, :, HD:] = values[rows, cols]
+    lax.fori_loop(1, early, functools.partial(heard, asked), 0)
+    asked_copy = pltpu.make_async_copy(asked, asked_here, asked_sem)
+    asked_copy.start()
+    asked_copy.wait()
+    lax.fori_loop(1, early, functools.partial(send_step, asked_here), 0)
+    lax.fori_loop(early, shards, functools.partial(ask, asked_late), 0)
+    for load in loads[2:]:
+        load.wait()
     for head in range(heads):
         cols = slice(head * HD, (head + 1) * HD)
         query_heads[head] = queries[:, cols]
         grad_heads[head] = grads[:, cols]
-        for block in range(blocks):
-            rows = slice(block * BLOCK, (block + 1) * BLOCK)
-            units_here[head * blocks + block, :, :HD] = keys[rows, cols]
-            units_here[head * blocks + block, :, HD:] = values[rows, cols]
-
-    def heard(target, _):
-        ask_copy(target, target, target, target).wait_recv()
-        return 0
-
-    lax.fori_loop(me + 1, shards, heard, 0)
-    asked_copy = pltpu.make_async_copy(asked, asked_here, asked_sem)
-    asked_copy.start()
-    asked_copy.wait()
     table_copy.wait()
-
-    def send(target):
-        for slot in range(CAP):
-            wanted = asked_here[target, 0, slot]
-            found = units_here[jnp.maximum(wanted, 0)]
-            outgoing[target, slot] = jnp.where(
-                jnp.full(found.shape, wanted, jnp.int32) >= 0, found, jnp.zeros_like(found)
-            )
-        pull_copy(target, me, target, me).start()
-
-    def send_step(step, _):
-        target = me + offset_of(step, shards)
-
-        @pl.when(target < shards)
-        def _():
-            send(target)
-
-        return 0
-
-    lax.fori_loop(1, min(WINDOW + 1, shards), send_step, 0)
+    lax.fori_loop(early, shards, functools.partial(heard, asked_late), 0)
+    late_copy = pltpu.make_async_copy(asked_late, asked_late_here, late_sem)
+    late_copy.start()
+    late_copy.wait()
     for head in range(heads):
         cols = slice(head * HD, (head + 1) * HD)
         products = grads[:, cols].astype(jnp.float32) * outputs[:, cols].astype(jnp.float32)
@@ -324,7 +359,13 @@
         @pl.when(target < shards)
         def _():
             back_copy(target, target, target, target).wait_recv()
-            first, second = (jnp.full((BLOCK, 2 * HD), asked_here[target, 0, i]) for i in range(CAP))
+            first, second = (
+                jnp.full(
+                    (BLOCK, 2 * HD),
+                    jnp.where(step < early, asked_here[target, 0, i], asked_late_here[target, 0, i]),
+                )
+                for i in range(CAP)
+            )
 
             def one_unit(unit, _):
                 late = jnp.where(second == unit, returned[target, 1].astype(jnp.float32), 0.0)
@@ -347,7 +388,7 @@
 
         @pl.when(step + WINDOW < shards)
         def _():
-            send_step(step + WINDOW, 0)
+            send_step(asked_late_here, step + WINDOW, 0)
 
         @pl.when(offset <= me)
         def _():
@@ -423,7 +464,7 @@
 
     def finish_requester(source, _):
         back_copy(source, source, source, source).wait_send()
-        ask_copy(source, source, source, source).wait_send()
+        ask_copy(asked, source, source, source, source).wait_send()
         return 0
 
     lax.fori_loop(0, me, finish_requester, 0)
@@ -434,6 +475,7 @@
         result[...] = given[...]
 
 
+HELD = pl.BlockSpec(memory_space=pl.ANY)
 VMEM = pl.BlockSpec(memory_space=pltpu.VMEM)
 
 
@@ -456,16 +498,19 @@
             result,
             result,
         ),
-        in_specs=[VMEM] * 7 + [pl.BlockSpec(memory_space=pl.ANY)],
+        in_specs=[VMEM] + [HELD] * 5 + [VMEM, HELD],
         out_specs=(VMEM,) * 3,
-        scratch_shapes=[
+        scratch_shapes=[pltpu.VMEM((tokens, width), jnp.bfloat16)] * 5
+        + [
             pltpu.VMEM((heads, 1, tokens), jnp.float32),
             pltpu.VMEM((heads, 1, tokens), jnp.float32),
             pltpu.VMEM((heads * blocks, BLOCK, 2 * HD), jnp.float32),
             pltpu.VMEM(paired, jnp.bfloat16),
             pltpu.VMEM((shards, 1, HD), jnp.int32),
+            pltpu.VMEM((shards, 1, HD), jnp.int32),
             pltpu.VMEM(paired, jnp.bfloat16),
             pltpu.VMEM((heads * blocks, BLOCK, 2 * HD), jnp.bfloat16),
+            pltpu.SMEM((shards, 1, HD), jnp.int32),
             pltpu.SMEM((shards, 1, HD), jnp.int32),
             pltpu.VMEM((shards, 1, HD), jnp.int32),
             pltpu.VMEM((8 + heads, HD), jnp.int32),
@@ -486,7 +531,8 @@
         + [pltpu.SemaphoreType.DMA((pieces, lanes_all)), pltpu.SemaphoreType.DMA((pieces, 2))]
         + [pltpu.SemaphoreType.DMA((pieces,))]
         + [pltpu.SemaphoreType.DMA((shards,))] * 2
-        + [pltpu.SemaphoreType.DMA] * 3,
+        + [pltpu.SemaphoreType.DMA] * 3
+        + [pltpu.SemaphoreType.DMA((5,)), pltpu.SemaphoreType.DMA],
         compiler_params=pltpu.CompilerParams(
             vmem_limit_bytes=56 * 2**20, collective_id=0, has_side_effects=True
         ),

time: 144 us -> 142 us (0.986)
  the two profiles are of different devices: /device:TPU:4 before, /device:TPU:34 now
where the time goes in v5:
time: 142 us
  Pallas kernels  141 us (99%)
    pallas_call x1, Pallas kernels, per_device(): pl.pallas_call(exchange_kernel, out_shape=(jax.ShapeDtypeStruct((stripe,...  139 us

profile of v5, /device:TPU:34, one launch (start us, length us, event | category | flops | bytes accessed | tf_op | source)
XLA Modules:
  0.0 142.1 jit_solution(9840782899826992290)
XLA Ops:
  0.6 138.9 %exchange.1 = (bf16[64,4096]{1,0:T(8,128)(2,1)}, bf16[256,1024]{1,0:T(8,128)(2,1)}, bf16[256,1024]{1,0:T(8,128)(2,1)}) custom-call(s32[8,4,16]{2,1,0:T(4,128)} %selected.1, bf16[256,1024]{1,0:T(8,128)(2,1)} %queries_far.1, bf16[256,1024]{1,0:T(8,128)(2,1)} %keys_far.1, bf16[256,1024]{1,0:T(8,128)(2,1)} %values_far.1, bf16[256,1024]{1,0:T(8,128)(2,1)} %outputs_far.1, ...), custom_call_target="tpu_custom_call" | custom-call | tf_op jit(solution)/shard_map/exchange/pallas_call | solution.py:494
  139.5 2.5 %hand_out.1 = (bf16[64,4096]{1,0:T(8,128)(2,1)}, bf16[256,1024]{1,0:T(8,128)(2,1)}, bf16[256,1024]{1,0:T(8,128)(2,1)}) custom-call(bf16[64,4096]{1,0:T(8,128)(2,1)} %get-tuple-element.6.refs_0_, bf16[256,1024]{1,0:T(8,128)(2,1)} %get-tuple-element.7.refs_1_, bf16[256,1024]{1,0:T(8,128)(2,1)} %get-tuple-element.8.refs_2_), custom_call_target="tpu_custom_call" | custom-call | tf_op jit(solution)/shard_map/hand_out/pallas_call | solution.py:550

commit v6 on v5

--- a/solution.py
+++ b/solution.py
@@ -378,16 +378,21 @@
 
         return 0
 
+    def sent_step(step, _):
+        sent = me + offset_of(step, shards)
+
+        @pl.when(sent < shards)
+        def _():
+            pull_copy(sent, sent, sent, sent).wait_send()
+
+        return 0
+
     def source_step(step, _):
         offset = offset_of(step, shards)
 
-        @pl.when(me + offset < shards)
-        def _():
-            sent = me + offset
-            pull_copy(sent, sent, sent, sent).wait_send()
-
         @pl.when(step + WINDOW < shards)
         def _():
+            sent_step(step, 0)
             send_step(asked_late_here, step + WINDOW, 0)
 
         @pl.when(offset <= me)
@@ -461,6 +466,8 @@
         return 0
 
     lax.fori_loop(0, pieces, one_sum, 0)
+
+    lax.fori_loop(max(1, shards - WINDOW), shards, sent_step, 0)
 
     def finish_requester(source, _):
         back_copy(source, source, source, source).wait_send()

time: 142 us -> 142 us (level); the launches traced: 142 us -> 140 us
    pallas_call x1, Pallas kernels: 139 us -> 137 us  [per_device(): pl.pallas_call(exchange_kernel, out_shape=(jax.ShapeDtypeStruct((stripe,...]
where the time goes in v6:
time: 142 us; the launch traced here: 140 us
  Pallas kernels  140 us (99%)
    pallas_call x1, Pallas kernels, per_device(): pl.pallas_call(exchange_kernel, out_shape=(jax.ShapeDtypeStruct((stripe,...  137 us

profile of v6, /device:TPU:34, one launch (start us, length us, event | category | flops | bytes accessed | tf_op | source)
XLA Modules:
  0.0 140.3 jit_solution(3608008432395152661)
XLA Ops:
  0.6 137.1 %exchange.1 = (bf16[64,4096]{1,0:T(8,128)(2,1)}, bf16[256,1024]{1,0:T(8,128)(2,1)}, bf16[256,1024]{1,0:T(8,128)(2,1)}) custom-call(s32[8,4,16]{2,1,0:T(4,128)} %selected.1, bf16[256,1024]{1,0:T(8,128)(2,1)} %queries_far.1, bf16[256,1024]{1,0:T(8,128)(2,1)} %keys_far.1, bf16[256,1024]{1,0:T(8,128)(2,1)} %values_far.1, bf16[256,1024]{1,0:T(8,128)(2,1)} %outputs_far.1, ...), custom_call_target="tpu_custom_call" | custom-call | tf_op jit(solution)/shard_map/exchange/pallas_call | solution.py:501
  137.7 2.5 %hand_out.1 = (bf16[64,4096]{1,0:T(8,128)(2,1)}, bf16[256,1024]{1,0:T(8,128)(2,1)}, bf16[256,1024]{1,0:T(8,128)(2,1)}) custom-call(bf16[64,4096]{1,0:T(8,128)(2,1)} %get-tuple-element.6.refs_0_, bf16[256,1024]{1,0:T(8,128)(2,1)} %get-tuple-element.7.refs_1_, bf16[256,1024]{1,0:T(8,128)(2,1)} %get-tuple-element.8.refs_2_), custom_call_target="tpu_custom_call" | custom-call | tf_op jit(solution)/shard_map/hand_out/pallas_call | solution.py:557

commit v7 on v6

--- a/solution.py
+++ b/solution.py
@@ -73,7 +73,7 @@
 
 
 def offset_of(step, shards):
-    return lax.rem(step * 27, shards)
+    return lax.rem(step * 19, shards)
 
 
 def exchange_kernel(

time: 142 us -> 141 us (level)
  no operation moved by 1% of the time
where the time goes in v7:
time: 141 us; the launch traced here: 139 us
  Pallas kernels  139 us (99%)
    pallas_call x1, Pallas kernels, per_device(): pl.pallas_call(exchange_kernel, out_shape=(jax.ShapeDtypeStruct((stripe,...  136 us

profile of v7, /device:TPU:34, one launch (start us, length us, event | category | flops | bytes accessed | tf_op | source)
XLA Modules:
  0.0 139.4 jit_solution(5205975080616359981)
XLA Ops:
  0.6 136.3 %exchange.1 = (bf16[64,4096]{1,0:T(8,128)(2,1)}, bf16[256,1024]{1,0:T(8,128)(2,1)}, bf16[256,1024]{1,0:T(8,128)(2,1)}) custom-call(s32[8,4,16]{2,1,0:T(4,128)} %selected.1, bf16[256,1024]{1,0:T(8,128)(2,1)} %queries_far.1, bf16[256,1024]{1,0:T(8,128)(2,1)} %keys_far.1, bf16[256,1024]{1,0:T(8,128)(2,1)} %values_far.1, bf16[256,1024]{1,0:T(8,128)(2,1)} %outputs_far.1, ...), custom_call_target="tpu_custom_call" | custom-call | tf_op jit(solution)/shard_map/exchange/pallas_call | solution.py:501
  136.9 2.5 %hand_out.1 = (bf16[64,4096]{1,0:T(8,128)(2,1)}, bf16[256,1024]{1,0:T(8,128)(2,1)}, bf16[256,1024]{1,0:T(8,128)(2,1)}) custom-call(bf16[64,4096]{1,0:T(8,128)(2,1)} %get-tuple-element.6.refs_0_, bf16[256,1024]{1,0:T(8,128)(2,1)} %get-tuple-element.7.refs_1_, bf16[256,1024]{1,0:T(8,128)(2,1)} %get-tuple-element.8.refs_2_), custom_call_target="tpu_custom_call" | custom-call | tf_op jit(solution)/shard_map/hand_out/pallas_call | solution.py:557
